TPU v7x, 256 devices: a whole 4x4x8 slice. The times are simulated.
256 devices in a mesh: grid: 64 (over z, y, core), rep: 4 (over x).
Axes of the slice: x: 4, y: 4, z: 8, core: 2. Of those that a mesh axis runs over, the one named last changes fastest.
Arguments:
- amplitudes: bfloat16 [22016, 4, 3072], P(None, 'rep', 'grid'), may hold values from -6 to 6
- integrals: bfloat16 [2048, 4, 3072], P(None, 'rep'), may hold values from -0.0546875 to 0.0546875
- rest_terms: bfloat16 [2048, 22016], P(('grid', 'rep')), may hold values from -6 to 6
- occupied_energy: float32 [150], replicated, may hold values from -1.5 to -0.3
- virtual_energy: float32 [900], replicated, may hold values from 0.1 to 3
- slab_start: int32 [1], replicated, may hold values from 0 to 807952
Outputs:
- new_amplitudes: bfloat16 [2048, 22016], P(('grid', 'rep'))
Inputs may be any that keep to these rules, and one draw needn't show every extreme that they name: `slab_start`: the slab lies within the 810000 virtual pairs.
All inputs are finite; a program needn't handle non-finite values.
Results may differ from a plain program's by a relative error of at most 0.0039.
Values may be sent and summed in bfloat16 or wider, within the bound.
No kernel may reach another device: no remote copies, remote signals or barrier semaphores. Data moves between devices by JAX's collectives and lax.ppermute only.
A program may use at most 128 MiB of HBM per device.

v0:
```python
import jax
import jax.numpy as jnp
from jax import lax
from jax.sharding import PartitionSpec as P


def on_device(amplitudes, integrals, rest_terms, occupied_energy, virtual_energy, slab_start):
    grid_size = lax.axis_size("grid")
    rep_size = lax.axis_size("rep")
    arrived = lax.all_to_all(amplitudes, "grid", split_axis=0, concat_axis=2, tiled=True)
    pair_rows = arrived[:, 0, :]
    weights = integrals[:, 0, :]
    slab_rows = weights.shape[0]
    share_rows = slab_rows // (grid_size * rep_size)
    block_rows = grid_size * share_rows
    split_weights = weights.reshape(grid_size, rep_size, share_rows, weights.shape[1])
    blocks = slab_rows // block_rows
    partial_term = jnp.einsum(
        "gsmk,ik->sgmi", split_weights, pair_rows, preferred_element_type=jnp.float32
    )
    summed_total = lax.psum(partial_term.reshape(blocks * block_rows, pair_rows.shape[0]), "rep")
    own_rows = lax.dynamic_slice_in_dim(
        summed_total, lax.axis_index("rep") * block_rows, block_rows, 0
    )
    ladder = lax.all_to_all(
        own_rows.astype(jnp.bfloat16), "grid", split_axis=0, concat_axis=1, tiled=True
    )
    pair_count = rest_terms.shape[1]
    occupied_count = occupied_energy.shape[0]
    virtual_count = virtual_energy.shape[0]
    occupied_sum = (occupied_energy[:, None] + occupied_energy[None, :]).reshape(
        occupied_count * occupied_count
    )[:pair_count]
    row_base = (lax.axis_index("grid") * rep_size + lax.axis_index("rep")) * share_rows
    pair_index = slab_start[0] + row_base + jnp.arange(share_rows, dtype=jnp.int32)
    first_orbital = pair_index // virtual_count
    second_orbital = pair_index % virtual_count
    orbital_ids = jnp.arange(virtual_count, dtype=jnp.int32)
    pick_first = first_orbital[:, None] == orbital_ids[None, :]
    pick_second = second_orbital[:, None] == orbital_ids[None, :]
    first_energy = jnp.sum(jnp.where(pick_first, virtual_energy[None, :], jnp.float32(0.0)), axis=1)
    second_energy = jnp.sum(
        jnp.where(pick_second, virtual_energy[None, :], jnp.float32(0.0)), axis=1
    )
    virtual_sum = first_energy + second_energy
    denominator = occupied_sum[None, :] - virtual_sum[:, None]
    updated = (ladder.astype(jnp.float32) + rest_terms.astype(jnp.float32)) / denominator
    return updated.astype(jnp.bfloat16)


def solution(mesh):
    placed = (P(None, "rep", "grid"), P(None, "rep", None), P(("grid", "rep"), None), P(), P(), P())
    return jax.shard_map(
        on_device, mesh=mesh, in_specs=placed, out_specs=P(("grid", "rep"), None), check_vma=False
    )
```

profile of v0, /device:TPU:6, one launch (start us, length us, event | category | flops | bytes accessed | tf_op | source)
XLA Modules:
  0.0 229.6 jit_solution(7601238185529940410)
XLA Ops:
  0.0 0.5 broadcast.54
  0.5 3.9 %reduce = bf16[22016,48]{0,1:T(8,128)(2,1)S(1)} reduce(bf16[22016,1,48]{0,2,1:T(8,128)(2,1)} %param.6, bf16[]{:T(256)} %broadcast.54), dimensions={1}, to_apply=%copy.31.reduce_sub_computation | reduce | bytes 4227074 | tf_op args[0]
  4.4 4.5 %copy.44 = bf16[22016,48]{1,0:T(8,128)(2,1)} copy(bf16[22016,48]{0,1:T(8,128)(2,1)S(1)} %reduce) | data formatting | bytes 4227072
  8.9 11.6 %reshape.43 = bf16[64,2,8256]{2,1,0:T(2,128)(2,1)} reshape(bf16[22016,48]{1,0:T(8,128)(2,1)} %copy.44) | data formatting | bytes 4227072
  20.5 12.3 %all-to-all-start = ((bf16[64,2,8256]{2,1,0:T(2,128)(2,1)}), bf16[64,2,8256]{2,1,0:T(2,128)(2,1)S(1)}, u32[]{:S(2)}, u32[]{:S(2)}) async-start(bf16[64,2,8256]{2,1,0:T(2,128)(2,1)} %reshape.43), calls=%async_computation | async-start | bytes 4259840 | tf_op jit(solution)/shard_map/all_to_all | solution.py:10
  32.8 51.9 %all-to-all-done = bf16[64,2,8256]{2,1,0:T(2,128)(2,1)S(1)} async-done(((bf16[64,2,8256]{2,1,0:T(2,128)(2,1)}), bf16[64,2,8256]{2,1,0:T(2,128)(2,1)S(1)}, u32[]{:S(2)}, u32[]{:S(2)}) %all-to-all-start) | async-done | bytes 2113568 | tf_op jit(solution)/shard_map/all_to_all | solution.py:10
  84.7 17.2 %reshape.44 = bf16[22016,1,48]{2,1,0:T(2,128)(2,1)} reshape(bf16[64,2,8256]{2,1,0:T(2,128)(2,1)S(1)} %all-to-all-done) | data formatting | bytes 4227072
  101.9 21.8 %copy.32 = bf16[22016,1,48]{0,2,1:T(8,128)(2,1)} copy(bf16[22016,1,48]{2,1,0:T(2,128)(2,1)} %reshape.44) | data formatting | bytes 4227072 | tf_op jit(solution)/shard_map/all_to_all | solution.py:10
  123.6 6.8 %all_to_all.22 = bf16[64,344,1,48]{1,0,3,2:T(8,128)(2,1)S(1)} reshape(bf16[22016,1,48]{0,2,1:T(8,128)(2,1)} %copy.32) | data formatting | bytes 4227072 | tf_op jit(solution)/shard_map/all_to_all | solution.py:10
  130.4 1.4 copy.33
  131.8 12.9 %fusion.2 = f32[4,64,8,344]{3,1,2,0:T(8,128)S(1)} fusion(bf16[344,3072,1,1]{0,1,3,2:T(8,128)(2,1)S(1)} %bitcast.20, bf16[64,4,8,3072]{3,2,1,0:T(8,128)(2,1)} %bitcast.22), kind=kOutput, calls=%fused_computation.2 | convolution fusion | flops 4328521728 | bytes 17514496 | tf_op jit(solution)/shard_map/gsmk,ik->sgmi/dot_general | solution.py:18
  144.7 1.8 copy.36
  146.5 0.0 copy-start.1
  146.5 56.9 %all-reduce.1 = bf16[2048,344]{1,0:T(8,128)(2,1)} all-reduce(f32[2048,344]{1,0:T(8,128)S(1)} %bitcast.18), channel_id=1, replica_groups=mesh['grid'=64,'rep'=4] {'rep'}, use_global_device_ids=true, to_apply=%region_0.0 | all-reduce | flops 704512 | bytes 4227072 | tf_op jit(solution)/shard_map/psum | solution.py:21
  203.4 1.8 fusion.5
  205.2 7.9 %all-to-all-start.1 = ((bf16[64,8,344]{2,1,0:T(8,128)(2,1)}), bf16[64,8,344]{2,1,0:T(8,128)(2,1)S(1)}, u32[]{:S(2)}, u32[]{:S(2)}) async-start(bf16[64,8,344]{2,1,0:T(8,128)(2,1)} %fusion.5), calls=%async_computation.1 | async-start | bytes 786432 | tf_op jit(solution)/shard_map/all_to_all | solution.py:25
  213.8 0.1 broadcast_add_fusion
  213.9 0.2 add.71
  214.2 0.2 select_reduce_fusion
  214.4 13.6 %all-to-all-done.1 = bf16[64,8,344]{2,1,0:T(8,128)(2,1)S(1)} async-done(((bf16[64,8,344]{2,1,0:T(8,128)(2,1)}), bf16[64,8,344]{2,1,0:T(8,128)(2,1)S(1)}, u32[]{:S(2)}, u32[]{:S(2)}) %all-to-all-start.1) | async-done | bytes 352288 | tf_op jit(solution)/shard_map/all_to_all | solution.py:25
  228.0 0.1 convert_bitcast_fusion
  228.0 0.2 copy.37
  228.2 0.4 reshape.41
  228.6 0.9 divide_convert_fusion
  (7 shorter events, 0.0 us)
Async XLA Ops:
  20.5 64.2 %all-to-all-start = ((bf16[64,2,8256]{2,1,0:T(2,128)(2,1)}), bf16[64,2,8256]{2,1,0:T(2,128)(2,1)S(1)}, u32[]{:S(2)}, u32[]{:S(2)}) async-start(bf16[64,2,8256]{2,1,0:T(2,128)(2,1)} %reshape.43), calls=%async_computation | async-start | bytes 4259840 | tf_op jit(solution)/shard_map/all_to_all | solution.py:10
  146.5 67.3 %copy-start.1 = (f32[150]{0:T(256)S(1)}, f32[150]{0:T(256)}, u32[]{:S(2)}) copy-start(f32[150]{0:T(256)} %param.9) | copy-start | bytes 1804
  146.5 67.6 %copy-start.2 = (f32[900]{0:T(1024)S(1)}, f32[900]{0:T(1024)}, u32[]{:S(2)}) copy-start(f32[900]{0:T(1024)} %param.10) | copy-start | bytes 10804
  205.2 22.8 %all-to-all-start.1 = ((bf16[64,8,344]{2,1,0:T(8,128)(2,1)}), bf16[64,8,344]{2,1,0:T(8,128)(2,1)S(1)}, u32[]{:S(2)}, u32[]{:S(2)}) async-start(bf16[64,8,344]{2,1,0:T(8,128)(2,1)} %fusion.5), calls=%async_computation.1 | async-start | bytes 786432 | tf_op jit(solution)/shard_map/all_to_all | solution.py:25
  213.1 15.5 %copy-start = (bf16[8,22016]{1,0:T(8,128)(2,1)S(1)}, bf16[8,22016]{1,0:T(8,128)(2,1)}, u32[]{:S(2)}) copy-start(bf16[8,22016]{1,0:T(8,128)(2,1)} %param.8) | copy-start | bytes 1056772
where the time goes:
time: 234 us; the launch traced here: 230 us
  local copies, waits for them, and re-layouts  68.1 us (29%)
  waiting for transfers between devices  65.5 us (28%)
  blocking collectives  56.9 us (24%)
  starting transfers between devices  20.2 us (9%)
  matrix products  12.9 us (6%)
  other arithmetic  5.18 us (2%)
    psum x1, blocking collectives, on_device(): lax.psum(partial_term.reshape(blocks * block_rows, pair_rows.shape[0]), '...  56.9 us
    all_to_all x1, waiting for transfers between devices, on_device(): lax.all_to_all(amplitudes, 'grid', split_axis=0, concat_axis=2, tiled=True)  51.9 us
    unnamed x10, local copies, waits for them, and re-layouts  33.8 us
    all_to_all x3, local copies, waits for them, and re-layouts, on_device(): lax.all_to_all(amplitudes, 'grid', split_axis=0, concat_axis=2, tiled=True)  29.9 us
    all_to_all x1, waiting for transfers between devices, on_device(): lax.all_to_all(own_rows.astype(jnp.bfloat16), 'grid', split_axis=0, conca...  13.6 us
    dot_general x1, matrix products, on_device(): jnp.einsum('gsmk,ik->sgmi', split_weights, pair_rows, preferred_element_t...  12.9 us
    all_to_all x1, starting transfers between devices, on_device(): lax.all_to_all(amplitudes, 'grid', split_axis=0, concat_axis=2, tiled=True)  12.3 us
    all_to_all x1, starting transfers between devices, on_device(): lax.all_to_all(own_rows.astype(jnp.bfloat16), 'grid', split_axis=0, conca...  7.87 us
  transfers between devices with their start and end apart: 2, of which 2 were waited for; matrix products, arithmetic and copies ran while one was open for 0% of the time, Pallas kernels for 0%

commit v1 on v0

v1 whole, which is shorter than its diff:
```python
import functools

import jax
import jax.numpy as jnp
from jax import lax
from jax.experimental import pallas as pl
from jax.experimental.pallas import tpu as pltpu
from jax.sharding import Mesh, PartitionSpec as P

Z, Y, CORES, REPS = 8, 4, 2, 4
CHIPS = Z * Y
TILE = 128
BF16, F32 = jnp.bfloat16, jnp.float32


def tile_starts(tiles, width):
    return [min(tiles * h // CHIPS, tiles - width) for h in range(CHIPS)]


def repack_kernel(starts, lanes, amp_ref, out_ref, sem):
    copies = [
        pltpu.make_async_copy(
            amp_ref.at[:, pl.ds(start * TILE, lanes)], out_ref.at[h], sem.at[h]
        )
        for h, start in enumerate(starts)
    ]
    for copy in copies:
        copy.start()
    for copy in copies:
        copy.wait()


def repack(amp, starts, lanes):
    return pl.pallas_call(
        functools.partial(repack_kernel, starts, lanes),
        out_shape=jax.ShapeDtypeStruct((CHIPS, amp.shape[0], lanes), amp.dtype),
        in_specs=[pl.BlockSpec(memory_space=pl.ANY)],
        out_specs=pl.BlockSpec(memory_space=pl.ANY),
        scratch_shapes=[pltpu.SemaphoreType.DMA((CHIPS,))],
    )(amp)


def matmul_kernel(
    place_ref, own_ref, other_ref, weight_ref, keep_ref, to1_ref, to2_ref, to3_ref, rows, total, sem
):
    core, rep = place_ref[0], place_ref[1]
    step = pl.program_id(0)

    @pl.when(step == 0)
    def _():
        first = pltpu.make_async_copy(own_ref, rows.at[:, core], sem.at[0])
        second = pltpu.make_async_copy(other_ref, rows.at[:, 1 - core], sem.at[1])
        first.start()
        second.start()
        first.wait()
        second.wait()

    lanes = total.shape[-1]
    depth = weight_ref.shape[-1]
    height = weight_ref.shape[0] * weight_ref.shape[2]
    weight = weight_ref[...].reshape(height, depth)
    for start in range(0, lanes, 256):
        part = rows[:, :, :, start : start + 256].reshape(depth, 256)
        term = jnp.dot(weight, part, preferred_element_type=F32)
        total[:, :, :, start : start + 256] = term.reshape(total.shape[:3] + (256,))
    block = keep_ref.shape
    keep_ref[...] = total[:, rep].reshape(block)
    for shift, ref in ((1, to1_ref), (2, to2_ref), (3, to3_ref)):
        ref[...] = total[:, lax.rem(rep + shift, REPS)].reshape(block).astype(BF16)


def matmul(place, own, other, weights, lanes):
    steps = 4
    chips = CHIPS // steps
    share = weights.shape[0] // (CHIPS * CORES * REPS)
    depth = weights.shape[1]
    split = weights.reshape(CHIPS, CORES, REPS * share, depth)
    sent = jax.ShapeDtypeStruct((CHIPS * share, lanes), BF16)
    block = pl.BlockSpec((chips * share, lanes), lambda i, place: (i, 0))
    return pl.pallas_call(
        matmul_kernel,
        grid_spec=pltpu.PrefetchScalarGridSpec(
            num_scalar_prefetch=1,
            grid=(steps,),
            in_specs=[
                pl.BlockSpec(memory_space=pl.ANY),
                pl.BlockSpec(memory_space=pl.ANY),
                pl.BlockSpec(
                    (chips, 1, REPS * share, depth), lambda i, place: (i, place[0], 0, 0)
                ),
            ],
            out_specs=[block] * 4,
            scratch_shapes=[
                pltpu.VMEM((CHIPS, CORES, own.shape[1], lanes), BF16),
                pltpu.VMEM((chips, REPS, share, lanes), F32),
                pltpu.SemaphoreType.DMA((2,)),
            ],
        ),
        out_shape=[jax.ShapeDtypeStruct(sent.shape, F32), sent, sent, sent],
        compiler_params=pltpu.CompilerParams(vmem_limit_bytes=40 * 1024 * 1024),
    )(place, own, other, split)


def update_kernel(starts, tiles, ladder_ref, rest_ref, occupied_ref, virtual_ref, out_ref):
    virtual_sum = virtual_ref[...]
    for h, start in enumerate(starts):
        stop = starts[h + 1] if h + 1 < CHIPS else tiles
        lanes = slice(start * TILE, stop * TILE)
        ladder = ladder_ref[h, :, : (stop - start) * TILE].astype(F32)
        denominator = occupied_ref[:, lanes] - virtual_sum
        out_ref[:, lanes] = ((ladder + rest_ref[:, lanes].astype(F32)) / denominator).astype(BF16)


def update(ladder, rest, occupied_sum, virtual_sum, starts):
    return pl.pallas_call(
        functools.partial(update_kernel, starts, rest.shape[1] // TILE),
        out_shape=jax.ShapeDtypeStruct(rest.shape, BF16),
        compiler_params=pltpu.CompilerParams(vmem_limit_bytes=16 * 1024 * 1024),
    )(ladder, rest, occupied_sum, virtual_sum)


def energy_sums(occupied, virtual, slab_start, pair_count, share):
    occupied_sum = (occupied[:, None] + occupied[None, :]).reshape(-1)[:pair_count]
    place = (lax.axis_index("z") * Y + lax.axis_index("y")) * CORES + lax.axis_index("core")
    row_base = (place * REPS + lax.axis_index("rep")) * share
    count = virtual.shape[0]
    pair_index = slab_start[0] + row_base + jnp.arange(share, dtype=jnp.int32)
    ids = jnp.arange(count, dtype=jnp.int32)
    pick_first = (pair_index // count)[:, None] == ids[None, :]
    pick_second = (pair_index % count)[:, None] == ids[None, :]
    zero = F32(0.0)
    first = jnp.sum(jnp.where(pick_first, virtual[None, :], zero), axis=1)
    second = jnp.sum(jnp.where(pick_second, virtual[None, :], zero), axis=1)
    return occupied_sum[None, :], (first + second)[:, None]


def shifted(array, axis, size, shift):
    return lax.ppermute(array, axis, [(i, (i + shift) % size) for i in range(size)])


def on_device(amplitudes, integrals, rest_terms, occupied_energy, virtual_energy, slab_start):
    amp = amplitudes[:, 0, :].T
    weights = integrals[:, 0, :]
    share, pair_count = rest_terms.shape
    tiles = pair_count // TILE
    width = -(-tiles // CHIPS)
    lanes = width * TILE
    starts = tile_starts(tiles, width)
    occupied_sum, virtual_sum = energy_sums(
        occupied_energy, virtual_energy, slab_start, pair_count, share
    )
    place = jnp.stack([lax.axis_index("core"), lax.axis_index("rep")]).astype(jnp.int32)

    sent = repack(amp, starts, lanes)
    own = lax.all_to_all(sent, ("z", "y"), split_axis=0, concat_axis=0, tiled=True)
    other = shifted(own, "core", CORES, 1)
    keep, to1, to2, to3 = matmul(place, own, other, weights, lanes)
    got2 = shifted(to2, "rep", REPS, 2)
    got1 = shifted(to1, "rep", REPS, 1)
    got3 = shifted(to3, "rep", REPS, 3)
    total = keep + got1.astype(F32) + got2.astype(F32) + got3.astype(F32)
    blocks = total.astype(BF16).reshape(CHIPS, share, lanes)
    ladder = lax.all_to_all(blocks, ("z", "y"), split_axis=0, concat_axis=0, tiled=True)
    return update(ladder, rest_terms, occupied_sum, virtual_sum, starts)


def solution(mesh):
    axes = ("z", "y", "core", "rep")
    split = Mesh(mesh.devices.reshape(Z, Y, CORES, REPS), axes)
    grid = axes[:3]
    placed = (P(None, "rep", grid), P(None, "rep", None), P(axes, None), P(), P(), P())
    return jax.shard_map(
        on_device, mesh=split, in_specs=placed, out_specs=P(axes, None), check_vma=False
    )
```

time: 234 us -> 201 us (0.86); the launches traced: 230 us -> 199 us
  Pallas kernels: 0 us -> 83.8 us
  local copies, waits for them, and re-layouts: 68.1 us -> 0.36 us
  waiting for transfers between devices: 65.5 us -> 35.5 us
  matrix products: 12.9 us -> 0 us
  blocking collectives: 56.9 us -> 69.2 us
  starting transfers between devices: 20.2 us -> 8.19 us
  other arithmetic: 5.18 us -> 1.32 us
    pallas_call x0 -> x3, Pallas kernels: none -> 83.8 us  [the longest x1 72.9 us: repack(): pl.pallas_call(functools.partial(repack_kernel, starts, lanes), out_shape...]
    all_to_all x0 -> x1, blocking collectives: none -> 69.2 us  [on_device(): lax.all_to_all(sent, ('z', 'y'), split_axis=0, concat_axis=0, tiled=True)]
    psum x1 -> x0, blocking collectives: 56.9 us -> none  [on_device(): lax.psum(partial_term.reshape(blocks * block_rows, pair_rows.shape[0]), '...]
    all_to_all x2 -> x1, waiting for transfers between devices: 65.5 us -> 13.6 us  [on_device(): lax.all_to_all(blocks, ('z', 'y'), split_axis=0, concat_axis=0, tiled=True)]
    unnamed x10 -> x6, local copies, waits for them, and re-layouts: 33.8 us -> 0.02 us
    all_to_all x4 -> x0, local copies, waits for them, and re-layouts: 31.7 us -> none  [the longest x3 29.9 us: on_device(): lax.all_to_all(amplitudes, 'grid', split_axis=0, concat_axis=2, tiled=True)]
    ppermute x0 -> x4, waiting for transfers between devices: none -> 21.9 us  [shifted(): lax.ppermute(array, axis, [(i, (i + shift) % size) for i in range(size)])]
    all_to_all x2 -> x1, starting transfers between devices: 20.2 us -> 4.01 us  [on_device(): lax.all_to_all(blocks, ('z', 'y'), split_axis=0, concat_axis=0, tiled=True)]
  transfers between devices with their start and end apart: 2 -> 5, of which waited for: 2 -> 4; matrix products, arithmetic and copies ran while one was open for 0% -> 0% of each run, Pallas kernels for 0% -> 0%
where the time goes in v1:
time: 201 us; the launch traced here: 199 us
  Pallas kernels  83.8 us (42%)
  blocking collectives  69.2 us (34%)
  waiting for transfers between devices  35.5 us (18%)
  starting transfers between devices  8.19 us (4%)
    pallas_call x1, Pallas kernels, repack(): pl.pallas_call(functools.partial(repack_kernel, starts, lanes), out_shape...  72.9 us
    all_to_all x1, blocking collectives, on_device(): lax.all_to_all(sent, ('z', 'y'), split_axis=0, concat_axis=0, tiled=True)  69.2 us
    ppermute x4, waiting for transfers between devices, shifted(): lax.ppermute(array, axis, [(i, (i + shift) % size) for i in range(size)])  21.9 us
    all_to_all x1, waiting for transfers between devices, on_device(): lax.all_to_all(blocks, ('z', 'y'), split_axis=0, concat_axis=0, tiled=True)  13.6 us
    pallas_call x1, Pallas kernels, matmul(): pl.pallas_call(matmul_kernel, grid_spec=pltpu.PrefetchScalarGridSpec(num_...  10 us
    ppermute x4, starting transfers between devices, shifted(): lax.ppermute(array, axis, [(i, (i + shift) % size) for i in range(size)])  4.18 us
  transfers between devices with their start and end apart: 5, of which 4 were waited for; matrix products, arithmetic and copies ran while one was open for 0% of the time, Pallas kernels for 0%

profile of v1, /device:TPU:6, one launch (start us, length us, event | category | flops | bytes accessed | tf_op | source)
XLA Modules:
  0.0 199.2 jit_solution(18427832506495726690)
XLA Ops:
  0.0 72.9 %shard_map.64 = bf16[32,48,768]{2,1,0:T(8,128)(2,1)} custom-call(bf16[48,22016]{1,0:T(8,128)(2,1)} %bitcast.14), custom_call_target="tpu_custom_call" | custom-call | tf_op jit(solution)/shard_map/pallas_call | solution.py:34
  72.9 69.2 %all_to_all.10.own_ref = bf16[32,48,768]{2,1,0:T(8,128)(2,1)S(1)} all-to-all(bf16[32,48,768]{2,1,0:T(8,128)(2,1)} %shard_map.64), channel_id=1, replica_groups=mesh['z'=8,'y'=4,'core'=2,'rep'=4] {'z','y'}, dimensions={0} | all-to-all | bytes 4718592 | tf_op jit(solution)/shard_map/all_to_all | solution.py:155
  142.1 0.0 collective-permute-start
  142.1 0.1 pad_add_fusion.place_ref
  142.2 4.6 %collective-permute-done.other_ref = bf16[32,48,768]{2,1,0:T(8,128)(2,1)} collective-permute-done((bf16[32,48,768]{2,1,0:T(8,128)(2,1)S(1)}, bf16[32,48,768]{2,1,0:T(8,128)(2,1)}, u32[]{:S(2)}, u32[]{:S(2)}) %collective-permute-start) | collective-permute-done | bytes 2359328 | tf_op jit(solution)/shard_map/ppermute | solution.py:138
  146.7 10.0 %shard_map.65 = (f32[256,768]{1,0:T(8,128)S(1)}, bf16[256,768]{1,0:T(8,128)(2,1)S(1)}, bf16[256,768]{1,0:T(8,128)(2,1)S(1)}, bf16[256,768]{1,0:T(8,128)(2,1)S(1)}) custom-call(s32[2]{0:T(128)S(1)} %pad_add_fusion.place_ref, bf16[32,48,768]{2,1,0:T(8,128)(2,1)S(1)} %all_to_all.10.own_ref, bf16[32,48,768]{2,1,0:T(8,128)(2,1)} %collective-permute-done.other_ref, ...), custom_call_target="tpu_custom_call" | custom-call | tf_op jit(solution)/shard_map/pallas_call | solution.py:80
  156.8 0.0 copy-start.1
  156.8 0.0 copy-start.2
  156.8 0.0 copy-start
  156.8 0.9 collective-permute-start.3
  157.7 1.1 collective-permute-start.2
  158.9 2.1 %collective-permute-start.1 = (bf16[256,768]{1,0:T(8,128)(2,1)S(1)}, bf16[256,768]{1,0:T(8,128)(2,1)S(1)}, u32[]{:S(2)}, u32[]{:S(2)}) collective-permute-start(bf16[256,768]{1,0:T(8,128)(2,1)S(1)} %get-tuple-element.10), channel_id=1, source_target_pairs={{0,1},{1,2},{2,3},{3,0},{4,5},{5,6},{6,7},{7,4},{8,9},{9,10},{10,1... | collective-permute-start | bytes 1179656 | tf_op jit(solution)/shard_map/ppermute | solution.py:138
  161.0 16.7 %collective-permute-done.3 = bf16[256,768]{1,0:T(8,128)(2,1)S(1)} collective-permute-done((bf16[256,768]{1,0:T(8,128)(2,1)S(1)}, bf16[256,768]{1,0:T(8,128)(2,1)S(1)}, u32[]{:S(2)}, u32[]{:S(2)}) %collective-permute-start.3) | collective-permute-done | bytes 393248 | tf_op jit(solution)/shard_map/ppermute | solution.py:138
  177.7 0.0 collective-permute-done.2
  177.7 0.6 collective-permute-done.1
  178.3 0.9 fusion
  179.2 4.0 %all-to-all-start.1 = ((bf16[32,8,768]{2,1,0:T(8,128)(2,1)}), bf16[32,8,768]{2,1,0:T(8,128)(2,1)S(1)}, u32[]{:S(2)}, u32[]{:S(2)}) async-start(bf16[32,8,768]{2,1,0:T(8,128)(2,1)} %fusion), calls=%async_computation.1 | async-start | bytes 786432 | tf_op jit(solution)/shard_map/all_to_all | solution.py:163
  183.2 0.1 broadcast_add_fusion
  183.3 0.2 add.85
  183.5 0.1 broadcast_in_dim.28.occupied_ref
  184.3 0.2 select_reduce_fusion
  184.5 0.1 copy.8.virtual_ref
  184.6 13.6 %all-to-all-done.1.ladder_ref = bf16[32,8,768]{2,1,0:T(8,128)(2,1)S(1)} async-done(((bf16[32,8,768]{2,1,0:T(8,128)(2,1)}), bf16[32,8,768]{2,1,0:T(8,128)(2,1)S(1)}, u32[]{:S(2)}, u32[]{:S(2)}) %all-to-all-start.1) | async-done | bytes 393248 | tf_op jit(solution)/shard_map/all_to_all | solution.py:163
  198.2 0.9 shard_map.66
  (5 shorter events, 0.0 us)
Async XLA Ops:
  142.1 4.7 %collective-permute-start = (bf16[32,48,768]{2,1,0:T(8,128)(2,1)S(1)}, bf16[32,48,768]{2,1,0:T(8,128)(2,1)}, u32[]{:S(2)}, u32[]{:S(2)}) collective-permute-start(bf16[32,48,768]{2,1,0:T(8,128)(2,1)S(1)} %all_to_all.10.own_ref), channel_id=1, source_target_pairs={{0,4},{4,0},{1,5},{5,1},{2,6},{6,2},{3,7},{7,3},{8,12},{12,8},{9,1... | collective-permute-start | bytes 7077896 | tf_op jit(solution)/shard_map/ppermute | solution.py:138
  156.8 26.5 %copy-start.1 = (f32[150]{0:T(256)S(1)}, f32[150]{0:T(256)}, u32[]{:S(2)}) copy-start(f32[150]{0:T(256)} %param.9) | copy-start | bytes 1804
  156.8 27.5 %copy-start.2 = (f32[900]{0:T(1024)S(1)}, f32[900]{0:T(1024)}, u32[]{:S(2)}) copy-start(f32[900]{0:T(1024)} %param.10) | copy-start | bytes 10804
  156.8 41.4 %copy-start = (bf16[8,22016]{1,0:T(8,128)(2,1)S(1)}, bf16[8,22016]{1,0:T(8,128)(2,1)}, u32[]{:S(2)}) copy-start(bf16[8,22016]{1,0:T(8,128)(2,1)} %rest_ref.1) | copy-start | bytes 1056772
  156.8 20.9 %collective-permute-start.3 = (bf16[256,768]{1,0:T(8,128)(2,1)S(1)}, bf16[256,768]{1,0:T(8,128)(2,1)S(1)}, u32[]{:S(2)}, u32[]{:S(2)}) collective-permute-start(bf16[256,768]{1,0:T(8,128)(2,1)S(1)} %get-tuple-element.12), channel_id=1, source_target_pairs={{0,3},{1,0},{2,1},{3,2},{4,7},{5,4},{6,5},{7,6},{8,11},{9,8},{10,9... | collective-permute-start | bytes 1179656 | tf_op jit(solution)/shard_map/ppermute | solution.py:138
  157.7 19.9 %collective-permute-start.2 = (bf16[256,768]{1,0:T(8,128)(2,1)S(1)}, bf16[256,768]{1,0:T(8,128)(2,1)S(1)}, u32[]{:S(2)}, u32[]{:S(2)}) collective-permute-start(bf16[256,768]{1,0:T(8,128)(2,1)S(1)} %get-tuple-element.11), channel_id=1, source_target_pairs={{0,2},{1,3},{2,0},{3,1},{4,6},{5,7},{6,4},{7,5},{8,10},{9,11},{10,... | collective-permute-start | bytes 1179656 | tf_op jit(solution)/shard_map/ppermute | solution.py:138
  158.9 19.4 %collective-permute-start.1 = (bf16[256,768]{1,0:T(8,128)(2,1)S(1)}, bf16[256,768]{1,0:T(8,128)(2,1)S(1)}, u32[]{:S(2)}, u32[]{:S(2)}) collective-permute-start(bf16[256,768]{1,0:T(8,128)(2,1)S(1)} %get-tuple-element.10), channel_id=1, source_target_pairs={{0,1},{1,2},{2,3},{3,0},{4,5},{5,6},{6,7},{7,4},{8,9},{9,10},{10,1... | collective-permute-start | bytes 1179656 | tf_op jit(solution)/shard_map/ppermute | solution.py:138
  179.2 19.0 %all-to-all-start.1 = ((bf16[32,8,768]{2,1,0:T(8,128)(2,1)}), bf16[32,8,768]{2,1,0:T(8,128)(2,1)S(1)}, u32[]{:S(2)}, u32[]{:S(2)}) async-start(bf16[32,8,768]{2,1,0:T(8,128)(2,1)} %fusion), calls=%async_computation.1 | async-start | bytes 786432 | tf_op jit(solution)/shard_map/all_to_all | solution.py:163

commit v2 on v0

v2 whole, which is shorter than its diff:
```python
import functools

import jax
import jax.numpy as jnp
from jax import lax
from jax.experimental import pallas as pl
from jax.experimental.pallas import tpu as pltpu
from jax.sharding import Mesh, PartitionSpec as P

Z, Y, CORES, REPS = 8, 4, 2, 4
CHIPS = Z * Y
TILE, HALF = 128, 64
WHOLE = 5
CHUNKS = ((0, 4), (4, 2))
BF16, F32 = jnp.bfloat16, jnp.float32
ANY = pl.BlockSpec(memory_space=pl.ANY)
VMEM = pl.BlockSpec(memory_space=pltpu.VMEM)
SMEM = pl.BlockSpec(memory_space=pltpu.SMEM)
LIMIT = pltpu.CompilerParams(vmem_limit_bytes=24 * 1024 * 1024)


class Plan:
    def __init__(self, tiles):
        self.tiles = tiles
        halves, share = 2 * tiles, 2 * WHOLE + 1
        starts = [min(halves * h // CHIPS, halves - share) for h in range(CHIPS)]
        self.odd = [start % 2 for start in starts]
        self.first = [start // 2 + start % 2 for start in starts]
        self.split = [start // 2 if start % 2 else start // 2 + WHOLE for start in starts]

    def sources(self):
        whole, half = {}, {}
        for h in range(CHIPS):
            for place in range(WHOLE):
                whole.setdefault(self.first[h] + place, (h, place))
            half[self.split[h], self.odd[h]] = h
        return [
            (whole[tile], None) if tile in whole else (None, (half[tile, 0], half[tile, 1]))
            for tile in range(self.tiles)
        ]


def swap_halves(block):
    return jnp.concatenate([block[:, HALF:], block[:, :HALF]], axis=1)


def repack_kernel(plan, amp_ref, out_ref):
    depth = amp_ref.shape[0]
    third = depth // 3
    low = lax.broadcasted_iota(jnp.int32, (third, TILE), 1) < HALF
    for h in range(CHIPS):
        for place in range(WHOLE):
            start = (plan.first[h] + place) * TILE
            out_ref[h, place * depth : (place + 1) * depth] = amp_ref[:, start : start + TILE]
        block = amp_ref[:, plan.split[h] * TILE : (plan.split[h] + 1) * TILE].astype(F32)
        other = swap_halves(block)
        if plan.odd[h]:
            block, other = other, block
        packed = jnp.where(low, block[:third], other[third : 2 * third])
        out_ref[h, WHOLE * depth : WHOLE * depth + third] = packed.astype(BF16)
        out_ref[h, WHOLE * depth + third : WHOLE * depth + 2 * third] = block[2 * third :].astype(BF16)


def repack(plan, amp):
    depth = amp.shape[0]
    return pl.pallas_call(
        functools.partial(repack_kernel, plan),
        out_shape=jax.ShapeDtypeStruct((CHIPS, WHOLE * depth + 2 * depth // 3, TILE), BF16),
        in_specs=[VMEM],
        out_specs=VMEM,
        compiler_params=LIMIT,
    )(amp)


def hold_kernel(place_ref, weight_ref, _, out_ref, sem):
    core = place_ref[2]
    copies = [
        pltpu.make_async_copy(weight_ref.at[h, core], out_ref.at[h], sem.at[h]) for h in range(CHIPS)
    ]
    for copy in copies:
        copy.start()
    for copy in copies:
        copy.wait()


def hold(place, weights, own):
    chips, _, height, depth = weights.shape
    return pl.pallas_call(
        hold_kernel,
        out_shape=jax.ShapeDtypeStruct((chips, height, depth), BF16),
        in_specs=[SMEM, ANY, ANY],
        out_specs=VMEM,
        scratch_shapes=[pltpu.SemaphoreType.DMA((chips,))],
        compiler_params=pltpu.CompilerParams(vmem_limit_bytes=14 * 1024 * 1024),
    )(place, pltpu.with_memory_space_constraint(weights, pltpu.HBM), own)


def tile_of(ref, place, depth):
    if place < WHOLE:
        return ref[:, place * depth : (place + 1) * depth]
    third = depth // 3
    packed = ref[:, WHOLE * depth : WHOLE * depth + third].astype(F32)
    swapped = jnp.concatenate([packed[:, :, HALF:], packed[:, :, :HALF]], axis=2)
    last = ref[:, WHOLE * depth + third : WHOLE * depth + 2 * third]
    return jnp.concatenate([packed.astype(BF16), swapped.astype(BF16), last], axis=1)


def matmul_kernel(
    chunk, place_ref, own_ref, other_ref, weight_ref, keep_ref, to1_ref, to2_ref, to3_ref, rows, total
):
    core, rep = place_ref[2], place_ref[3]
    chips, share = total.shape[0], total.shape[2]
    height = chips * weight_ref.shape[1]
    depth = weight_ref.shape[2]
    block = chips * share
    first = core == 0
    for i in range(chunk[1]):
        own = tile_of(own_ref, chunk[0] + i, rows.shape[2])
        other = tile_of(other_ref, chunk[0] + i, rows.shape[2])
        lanes = slice(i * TILE, (i + 1) * TILE)
        rows[:, 0, :, lanes] = jnp.where(first, own, other)
        rows[:, 1, :, lanes] = jnp.where(first, other, own)
    step = total.shape[3]
    for i in range(CHIPS // chips):
        left = weight_ref[i * chips : (i + 1) * chips].reshape(height, depth)
        here = slice(i * block, (i + 1) * block)
        for start in range(0, rows.shape[3], step):
            lanes = slice(start, start + step)
            right = rows[:, :, :, lanes].reshape(depth, step)
            term = jnp.dot(left, right, preferred_element_type=F32)
            total[...] = term.reshape(total.shape)
            keep_ref[here, lanes] = total[:, pl.ds(rep, 1)].reshape(block, step)
            for shift, ref in ((1, to1_ref), (2, to2_ref), (3, to3_ref)):
                sent = total[:, pl.ds(lax.rem(rep + shift, REPS), 1)].reshape(block, step)
                ref[here, lanes] = sent.astype(BF16)


def matmul(chunk, place, own, other, weights):
    chips, height, depth = weights.shape
    share = height // REPS
    lanes = chunk[1] * TILE
    shape = (CHIPS * share, lanes)
    return pl.pallas_call(
        functools.partial(matmul_kernel, chunk),
        out_shape=[jax.ShapeDtypeStruct(shape, F32)] + [jax.ShapeDtypeStruct(shape, BF16)] * 3,
        in_specs=[SMEM] + [VMEM] * 3,
        out_specs=[VMEM] * 4,
        scratch_shapes=[
            pltpu.VMEM((CHIPS, CORES, depth // (CHIPS * CORES), lanes), BF16),
            pltpu.VMEM((8, REPS, share, 2 * TILE), F32),
        ],
        compiler_params=LIMIT,
        cost_estimate=pl.CostEstimate(
            flops=2 * chips * height * depth * lanes,
            bytes_accessed=2 * chips * height * depth,
            transcendentals=0,
        ),
    )(place, own, other, weights)


def update_kernel(plan, ladder_ref, rest_ref, occupied_ref, virtual_ref, out_ref):
    virtual_sum = virtual_ref[...]
    low = lax.broadcasted_iota(jnp.int32, (ladder_ref.shape[1], TILE), 1) < HALF
    half = slice(WHOLE * TILE, (WHOLE + 1) * TILE)
    for tile, (whole, halves) in enumerate(plan.sources()):
        lanes = slice(tile * TILE, (tile + 1) * TILE)
        if whole is not None:
            h, place = whole
            ladder = ladder_ref[h, :, place * TILE : (place + 1) * TILE].astype(F32)
        else:
            left, right = (ladder_ref[h, :, half].astype(F32) for h in halves)
            ladder = jnp.where(low, left, swap_halves(right))
        denominator = occupied_ref[:, lanes] - virtual_sum
        total = ladder + rest_ref[:, lanes].astype(F32)
        out_ref[:, lanes] = (total / denominator).astype(BF16)


def update(plan, ladder, rest, occupied_sum, virtual_sum):
    return pl.pallas_call(
        functools.partial(update_kernel, plan),
        out_shape=jax.ShapeDtypeStruct(rest.shape, BF16),
        compiler_params=LIMIT,
    )(ladder, rest, occupied_sum, virtual_sum)


def energy_sums(occupied, virtual, slab_start, pair_count, share):
    occupied_sum = (occupied[:, None] + occupied[None, :]).reshape(-1)[:pair_count]
    place = (lax.axis_index("z") * Y + lax.axis_index("y")) * CORES + lax.axis_index("core")
    row_base = (place * REPS + lax.axis_index("rep")) * share
    count = virtual.shape[0]
    pair_index = slab_start[0] + row_base + jnp.arange(share, dtype=jnp.int32)
    ids = jnp.arange(count, dtype=jnp.int32)
    pick_first = (pair_index // count)[:, None] == ids[None, :]
    pick_second = (pair_index % count)[:, None] == ids[None, :]
    zero = F32(0.0)
    first = jnp.sum(jnp.where(pick_first, virtual[None, :], zero), axis=1)
    second = jnp.sum(jnp.where(pick_second, virtual[None, :], zero), axis=1)
    return occupied_sum[None, :], (first + second)[:, None]


def shifted(array, axis, size, shift):
    return lax.ppermute(array, axis, [(i, (i + shift) % size) for i in range(size)])


def after(array, others):
    return lax.optimization_barrier((array, *others))[0]


def over_rep(chunk, place, own, other, weights):
    keep, to1, to2, to3 = matmul(chunk, place, own, other, weights)
    got2 = shifted(to2, "rep", REPS, 2)
    got1 = shifted(to1, "rep", REPS, 1)
    got3 = shifted(to3, "rep", REPS, 3)
    total = keep + got1.astype(F32) + got2.astype(F32) + got3.astype(F32)
    return total.astype(BF16)


def on_device(amplitudes, integrals, rest_terms, occupied_energy, virtual_energy, slab_start):
    amp = amplitudes[:, 0, :].T
    share, pair_count = rest_terms.shape
    plan = Plan(pair_count // TILE)
    occupied_sum, virtual_sum = energy_sums(
        occupied_energy, virtual_energy, slab_start, pair_count, share
    )
    place = jnp.stack([lax.axis_index(a) for a in ("z", "y", "core", "rep")]).astype(jnp.int32)
    split = integrals.reshape(CHIPS, CORES, REPS * share, integrals.shape[2])

    own = lax.all_to_all(repack(plan, amp), ("z", "y"), split_axis=0, concat_axis=0, tiled=True)
    other = shifted(own, "core", CORES, 1)
    weights = hold(place, split, own)
    totals = [over_rep(chunk, place, own, other, weights) for chunk in CHUNKS]
    total = jnp.concatenate(totals, axis=1)
    ladder = lax.all_to_all(
        total.reshape(CHIPS, share, -1), ("z", "y"), split_axis=0, concat_axis=0, tiled=True
    )
    return update(plan, ladder, rest_terms, occupied_sum, virtual_sum)


def solution(mesh):
    axes = ("z", "y", "core", "rep")
    split = Mesh(mesh.devices.reshape(Z, Y, CORES, REPS), axes)
    grid = axes[:3]
    placed = (P(None, "rep", grid), P(None, "rep", None), P(axes, None), P(), P(), P())
    return jax.shard_map(
        on_device, mesh=split, in_specs=placed, out_specs=P(axes, None), check_vma=False
    )
```

time: 234 us -> 125 us (0.53)
  local copies, waits for them, and re-layouts: 68.1 us -> 1.95 us
  waiting for transfers between devices: 65.5 us -> 24.5 us
  Pallas kernels: 0 us -> 14.2 us
  matrix products: 12.9 us -> 0 us
  blocking collectives: 56.9 us -> 66.7 us
  starting transfers between devices: 20.2 us -> 12.8 us
  other arithmetic: 5.18 us -> 1.41 us
    all_to_all x0 -> x1, blocking collectives: none -> 66.7 us  [on_device(): lax.all_to_all(repack(plan, amp), ('z', 'y'), split_axis=0, concat_axis=0...]
    psum x1 -> x0, blocking collectives: 56.9 us -> none  [on_device(): lax.psum(partial_term.reshape(blocks * block_rows, pair_rows.shape[0]), '...]
    all_to_all x2 -> x1, waiting for transfers between devices: 65.5 us -> 13.7 us  [on_device(): lax.all_to_all(total.reshape(CHIPS, share, -1), ('z', 'y'), split_axis=0,...]
    unnamed x10 -> x8, local copies, waits for them, and re-layouts: 33.8 us -> 1.61 us
    all_to_all x4 -> x0, local copies, waits for them, and re-layouts: 31.7 us -> none  [the longest x3 29.9 us: on_device(): lax.all_to_all(amplitudes, 'grid', split_axis=0, concat_axis=2, tiled=True)]
    all_to_all x2 -> x1, starting transfers between devices: 20.2 us -> 3.88 us  [on_device(): lax.all_to_all(total.reshape(CHIPS, share, -1), ('z', 'y'), split_axis=0,...]
    pallas_call x0 -> x5, Pallas kernels: none -> 14.2 us  [the longest x2 9.22 us: matmul(): pl.pallas_call(functools.partial(matmul_kernel, chunk), out_shape=[jax.Sh...]
    dot_general x1 -> x0, matrix products: 12.9 us -> none  [on_device(): jnp.einsum('gsmk,ik->sgmi', split_weights, pair_rows, preferred_element_t...]
  transfers between devices with their start and end apart: 2 -> 8, of which waited for: 2 -> 4; matrix products, arithmetic and copies ran while one was open for 0% -> 1% of each run, Pallas kernels for 0% -> 8%
where the time goes in v2:
time: 125 us; the launch traced here: 122 us
  blocking collectives  66.7 us (53%)
  waiting for transfers between devices  24.5 us (20%)
  Pallas kernels  14.2 us (11%)
  starting transfers between devices  12.8 us (10%)
  local copies, waits for them, and re-layouts  1.95 us (2%)
  other arithmetic  1.41 us (1%)
    all_to_all x1, blocking collectives, on_device(): lax.all_to_all(repack(plan, amp), ('z', 'y'), split_axis=0, concat_axis=0...  66.7 us
    all_to_all x1, waiting for transfers between devices, on_device(): lax.all_to_all(total.reshape(CHIPS, share, -1), ('z', 'y'), split_axis=0,...  13.7 us
    ppermute x7, waiting for transfers between devices, shifted(): lax.ppermute(array, axis, [(i, (i + shift) % size) for i in range(size)])  10.8 us
    pallas_call x2, Pallas kernels, matmul(): pl.pallas_call(functools.partial(matmul_kernel, chunk), out_shape=[jax.Sh...  9.22 us
    ppermute x7, starting transfers between devices, shifted(): lax.ppermute(array, axis, [(i, (i + shift) % size) for i in range(size)])  8.97 us
    all_to_all x1, starting transfers between devices, on_device(): lax.all_to_all(total.reshape(CHIPS, share, -1), ('z', 'y'), split_axis=0,...  3.88 us
    pallas_call x1, Pallas kernels, hold(): pl.pallas_call(hold_kernel, out_shape=jax.ShapeDtypeStruct((chips, height...  3.7 us
  transfers between devices with their start and end apart: 8, of which 4 were waited for; matrix products, arithmetic and copies ran while one was open for 1% of the time, Pallas kernels for 8%

profile of v2, /device:TPU:6, one launch (start us, length us, event | category | flops | bytes accessed | tf_op | source)
XLA Modules:
  0.0 122.5 jit_solution(9737149608783993921)
XLA Ops:
  0.0 1.6 %copy-done = bf16[22016,1,48]{0,2,1:T(8,128)(2,1)S(1)} copy-done((bf16[22016,1,48]{0,2,1:T(8,128)(2,1)S(1)}, bf16[22016,1,48]{0,2,1:T(8,128)(2,1)}, u32[]{:S(2)}) %copy-start) | copy-done | bytes 2113560
  1.6 0.4 shard_map.64
  2.0 66.7 %all_to_all.10._.own_ref = bf16[32,272,128]{2,1,0:T(8,128)(2,1)S(1)} all-to-all(bf16[32,272,128]{2,1,0:T(8,128)(2,1)S(1)} %shard_map.64), channel_id=1, replica_groups=mesh['z'=8,'y'=4,'core'=2,'rep'=4] {'z','y'}, dimensions={0} | all-to-all | bytes 4456448 | tf_op jit(solution)/shard_map/all_to_all | solution.py:228
  68.8 3.7 %shard_map.65.weight_ref = bf16[32,32,3072]{2,1,0:T(8,128)(2,1)S(1)} custom-call(s32[4]{0:T(128)S(1)} %pad_add_fusion.place_ref, bf16[32,2,32,3072]{3,2,1,0:T(8,128)(2,1)} %bitcast.16, bf16[32,272,128]{2,1,0:T(8,128)(2,1)S(1)} %all_to_all.10._.own_ref), custom_call_target="tpu_custom_call" | custom-call | tf_op jit(solution)/shard_map/pallas_call | solution.py:88
  72.5 0.7 collective-permute-done.other_ref
  73.2 3.7 %shard_map.67 = (f32[256,256]{1,0:T(8,128)S(1)}, bf16[256,256]{1,0:T(8,128)(2,1)S(1)}, bf16[256,256]{1,0:T(8,128)(2,1)S(1)}, bf16[256,256]{1,0:T(8,128)(2,1)S(1)}) custom-call(s32[4]{0:T(128)S(1)} %pad_add_fusion.place_ref, bf16[32,272,128]{2,1,0:T(8,128)(2,1)S(1)} %all_to_all.10._.own_ref, bf16[32,272,128]{2,1,0:T(8,128)(2,1)} %collective-permute-done.other_ref, ...), custom_call_target="tpu_custom_call" | custom-call | flops 1610612736 | bytes 6291456 | tf_op jit(solution)/shard_map/pallas_call | solution.py:143
  76.9 0.9 collective-permute-start.6
  77.8 1.1 collective-permute-start.5
  78.9 2.1 %collective-permute-start.4 = (bf16[256,256]{1,0:T(8,128)(2,1)S(1)}, bf16[256,256]{1,0:T(8,128)(2,1)S(1)}, u32[]{:S(2)}, u32[]{:S(2)}) collective-permute-start(bf16[256,256]{1,0:T(8,128)(2,1)S(1)} %get-tuple-element.18), channel_id=1, source_target_pairs={{0,1},{1,2},{2,3},{3,0},{4,5},{5,6},{6,7},{7,4},{8,9},{9,10},{10,1... | collective-permute-start | bytes 393224 | tf_op jit(solution)/shard_map/ppermute | solution.py:202
  81.0 5.5 %shard_map.66 = (f32[256,512]{1,0:T(8,128)S(1)}, bf16[256,512]{1,0:T(8,128)(2,1)S(1)}, bf16[256,512]{1,0:T(8,128)(2,1)S(1)}, bf16[256,512]{1,0:T(8,128)(2,1)S(1)}) custom-call(s32[4]{0:T(128)S(1)} %pad_add_fusion.place_ref, bf16[32,272,128]{2,1,0:T(8,128)(2,1)S(1)} %all_to_all.10._.own_ref, bf16[32,272,128]{2,1,0:T(8,128)(2,1)} %collective-permute-done.other_ref, ...), custom_call_target="tpu_custom_call" | custom-call | flops 3221225472 | bytes 6291456 | tf_op jit(solution)/shard_map/pallas_call | solution.py:143
  86.6 0.1 collective-permute-start.3
  86.7 2.3 %collective-permute-start.2 = (bf16[256,512]{1,0:T(8,128)(2,1)S(1)}, bf16[256,512]{1,0:T(8,128)(2,1)S(1)}, u32[]{:S(2)}, u32[]{:S(2)}) collective-permute-start(bf16[256,512]{1,0:T(8,128)(2,1)S(1)} %get-tuple-element.15), channel_id=1, source_target_pairs={{0,2},{1,3},{2,0},{3,1},{4,6},{5,7},{6,4},{7,5},{8,10},{9,11},{10,... | collective-permute-start | bytes 786440 | tf_op jit(solution)/shard_map/ppermute | solution.py:202
  89.0 2.4 %collective-permute-start.1 = (bf16[256,512]{1,0:T(8,128)(2,1)S(1)}, bf16[256,512]{1,0:T(8,128)(2,1)S(1)}, u32[]{:S(2)}, u32[]{:S(2)}) collective-permute-start(bf16[256,512]{1,0:T(8,128)(2,1)S(1)} %get-tuple-element.14), channel_id=1, source_target_pairs={{0,1},{1,2},{2,3},{3,0},{4,5},{5,6},{6,7},{7,4},{8,9},{9,10},{10,1... | collective-permute-start | bytes 786440 | tf_op jit(solution)/shard_map/ppermute | solution.py:202
  91.5 9.5 %collective-permute-done.3 = bf16[256,512]{1,0:T(8,128)(2,1)S(1)} collective-permute-done((bf16[256,512]{1,0:T(8,128)(2,1)S(1)}, bf16[256,512]{1,0:T(8,128)(2,1)S(1)}, u32[]{:S(2)}, u32[]{:S(2)}) %collective-permute-start.3) | collective-permute-done | bytes 262176 | tf_op jit(solution)/shard_map/ppermute | solution.py:202
  101.0 0.6 collective-permute-done.1
  101.6 0.2 add_convert_fusion
  101.8 0.8 maximum_bitcast_fusion
  102.5 3.9 %all-to-all-start.1 = ((bf16[32,8,768]{2,1,0:T(8,128)(2,1)}), bf16[32,8,768]{2,1,0:T(8,128)(2,1)S(1)}, u32[]{:S(2)}, u32[]{:S(2)}) async-start(bf16[32,8,768]{2,1,0:T(8,128)(2,1)} %maximum_bitcast_fusion), calls=%async_computation.1 | async-start | bytes 786432 | tf_op jit(solution)/shard_map/all_to_all | solution.py:233
  106.4 0.1 broadcast_add_fusion
  106.5 0.2 add.97
  107.5 0.2 select_reduce_fusion
  107.7 0.1 copy.8.virtual_ref
  107.8 13.7 %all-to-all-done.1.ladder_ref = bf16[32,8,768]{2,1,0:T(8,128)(2,1)S(1)} async-done(((bf16[32,8,768]{2,1,0:T(8,128)(2,1)}), bf16[32,8,768]{2,1,0:T(8,128)(2,1)S(1)}, u32[]{:S(2)}, u32[]{:S(2)}) %all-to-all-start.1) | async-done | bytes 393248 | tf_op jit(solution)/shard_map/all_to_all | solution.py:233
  121.5 0.9 shard_map.68
  (17 shorter events, 0.3 us)
Async XLA Ops:
  0.0 1.6 %copy-start = (bf16[22016,1,48]{0,2,1:T(8,128)(2,1)S(1)}, bf16[22016,1,48]{0,2,1:T(8,128)(2,1)}, u32[]{:S(2)}) copy-start(bf16[22016,1,48]{0,2,1:T(8,128)(2,1)} %param.6) | copy-start | bytes 6340612
  68.7 4.5 %collective-permute-start = (bf16[32,272,128]{2,1,0:T(8,128)(2,1)S(1)}, bf16[32,272,128]{2,1,0:T(8,128)(2,1)}, u32[]{:S(2)}, u32[]{:S(2)}) collective-permute-start(bf16[32,272,128]{2,1,0:T(8,128)(2,1)S(1)} %all_to_all.10._.own_ref), channel_id=1, source_target_pairs={{0,4},{4,0},{1,5},{5,1},{2,6},{6,2},{3,7},{7,3},{8,12},{12,8},{9,1... | collective-permute-start | bytes 6684680 | tf_op jit(solution)/shard_map/ppermute | solution.py:202
  76.9 12.1 %collective-permute-start.6 = (bf16[256,256]{1,0:T(8,128)(2,1)S(1)}, bf16[256,256]{1,0:T(8,128)(2,1)S(1)}, u32[]{:S(2)}, u32[]{:S(2)}) collective-permute-start(bf16[256,256]{1,0:T(8,128)(2,1)S(1)} %get-tuple-element.20), channel_id=1, source_target_pairs={{0,3},{1,0},{2,1},{3,2},{4,7},{5,4},{6,5},{7,6},{8,11},{9,8},{10,9... | collective-permute-start | bytes 393224 | tf_op jit(solution)/shard_map/ppermute | solution.py:202
  77.8 13.6 %collective-permute-start.5 = (bf16[256,256]{1,0:T(8,128)(2,1)S(1)}, bf16[256,256]{1,0:T(8,128)(2,1)S(1)}, u32[]{:S(2)}, u32[]{:S(2)}) collective-permute-start(bf16[256,256]{1,0:T(8,128)(2,1)S(1)} %get-tuple-element.19), channel_id=1, source_target_pairs={{0,2},{1,3},{2,0},{3,1},{4,6},{5,7},{6,4},{7,5},{8,10},{9,11},{10,... | collective-permute-start | bytes 393224 | tf_op jit(solution)/shard_map/ppermute | solution.py:202
  78.9 12.5 %collective-permute-start.4 = (bf16[256,256]{1,0:T(8,128)(2,1)S(1)}, bf16[256,256]{1,0:T(8,128)(2,1)S(1)}, u32[]{:S(2)}, u32[]{:S(2)}) collective-permute-start(bf16[256,256]{1,0:T(8,128)(2,1)S(1)} %get-tuple-element.18), channel_id=1, source_target_pairs={{0,1},{1,2},{2,3},{3,0},{4,5},{5,6},{6,7},{7,4},{8,9},{9,10},{10,1... | collective-permute-start | bytes 393224 | tf_op jit(solution)/shard_map/ppermute | solution.py:202
  86.6 19.9 %copy-start.2 = (f32[150]{0:T(256)S(1)}, f32[150]{0:T(256)}, u32[]{:S(2)}) copy-start(f32[150]{0:T(256)} %param.9) | copy-start | bytes 1804
  86.6 14.4 %collective-permute-start.3 = (bf16[256,512]{1,0:T(8,128)(2,1)S(1)}, bf16[256,512]{1,0:T(8,128)(2,1)S(1)}, u32[]{:S(2)}, u32[]{:S(2)}) collective-permute-start(bf16[256,512]{1,0:T(8,128)(2,1)S(1)} %get-tuple-element.16), channel_id=1, source_target_pairs={{0,3},{1,0},{2,1},{3,2},{4,7},{5,4},{6,5},{7,6},{8,11},{9,8},{10,9... | collective-permute-start | bytes 786440 | tf_op jit(solution)/shard_map/ppermute | solution.py:202
  86.7 14.3 %collective-permute-start.2 = (bf16[256,512]{1,0:T(8,128)(2,1)S(1)}, bf16[256,512]{1,0:T(8,128)(2,1)S(1)}, u32[]{:S(2)}, u32[]{:S(2)}) collective-permute-start(bf16[256,512]{1,0:T(8,128)(2,1)S(1)} %get-tuple-element.15), channel_id=1, source_target_pairs={{0,2},{1,3},{2,0},{3,1},{4,6},{5,7},{6,4},{7,5},{8,10},{9,11},{10,... | collective-permute-start | bytes 786440 | tf_op jit(solution)/shard_map/ppermute | solution.py:202
  89.0 12.6 %collective-permute-start.1 = (bf16[256,512]{1,0:T(8,128)(2,1)S(1)}, bf16[256,512]{1,0:T(8,128)(2,1)S(1)}, u32[]{:S(2)}, u32[]{:S(2)}) collective-permute-start(bf16[256,512]{1,0:T(8,128)(2,1)S(1)} %get-tuple-element.14), channel_id=1, source_target_pairs={{0,1},{1,2},{2,3},{3,0},{4,5},{5,6},{6,7},{7,4},{8,9},{9,10},{10,1... | collective-permute-start | bytes 786440 | tf_op jit(solution)/shard_map/ppermute | solution.py:202
  91.4 16.1 %copy-start.3 = (f32[900]{0:T(1024)S(1)}, f32[900]{0:T(1024)}, u32[]{:S(2)}) copy-start(f32[900]{0:T(1024)} %param.10) | copy-start | bytes 10804
  91.4 30.1 %copy-start.1 = (bf16[8,22016]{1,0:T(8,128)(2,1)S(1)}, bf16[8,22016]{1,0:T(8,128)(2,1)}, u32[]{:S(2)}) copy-start(bf16[8,22016]{1,0:T(8,128)(2,1)} %rest_ref.1) | copy-start | bytes 1056772
  102.5 19.0 %all-to-all-start.1 = ((bf16[32,8,768]{2,1,0:T(8,128)(2,1)}), bf16[32,8,768]{2,1,0:T(8,128)(2,1)S(1)}, u32[]{:S(2)}, u32[]{:S(2)}) async-start(bf16[32,8,768]{2,1,0:T(8,128)(2,1)} %maximum_bitcast_fusion), calls=%async_computation.1 | async-start | bytes 786432 | tf_op jit(solution)/shard_map/all_to_all | solution.py:233

commit v3 on v2

--- a/solution.py
+++ b/solution.py
@@ -11,7 +11,8 @@
 CHIPS = Z * Y
 TILE, HALF = 128, 64
 WHOLE = 5
-CHUNKS = ((0, 4), (4, 2))
+TILES = WHOLE + 1
+STEP = 2 * TILE
 BF16, F32 = jnp.bfloat16, jnp.float32
 ANY = pl.BlockSpec(memory_space=pl.ANY)
 VMEM = pl.BlockSpec(memory_space=pltpu.VMEM)
@@ -73,9 +74,12 @@
 
 
 def hold_kernel(place_ref, weight_ref, _, out_ref, sem):
-    core = place_ref[2]
+    core, rep = place_ref[2], place_ref[3]
     copies = [
-        pltpu.make_async_copy(weight_ref.at[h, core], out_ref.at[h], sem.at[h]) for h in range(CHIPS)
+        pltpu.make_async_copy(
+            weight_ref.at[:, core, lax.rem(rep + k, REPS)], out_ref.at[k], sem.at[k]
+        )
+        for k in range(REPS)
     ]
     for copy in copies:
         copy.start()
@@ -84,14 +88,14 @@
 
 
 def hold(place, weights, own):
-    chips, _, height, depth = weights.shape
+    chips, _, _, share, depth = weights.shape
     return pl.pallas_call(
         hold_kernel,
-        out_shape=jax.ShapeDtypeStruct((chips, height, depth), BF16),
+        out_shape=jax.ShapeDtypeStruct((REPS, chips, share, depth), BF16),
         in_specs=[SMEM, ANY, ANY],
         out_specs=VMEM,
-        scratch_shapes=[pltpu.SemaphoreType.DMA((chips,))],
-        compiler_params=pltpu.CompilerParams(vmem_limit_bytes=14 * 1024 * 1024),
+        scratch_shapes=[pltpu.SemaphoreType.DMA((REPS,))],
+        compiler_params=LIMIT,
     )(place, pltpu.with_memory_space_constraint(weights, pltpu.HBM), own)
 
 
@@ -105,57 +109,76 @@
     return jnp.concatenate([packed.astype(BF16), swapped.astype(BF16), last], axis=1)
 
 
-def matmul_kernel(
-    chunk, place_ref, own_ref, other_ref, weight_ref, keep_ref, to1_ref, to2_ref, to3_ref, rows, total
-):
-    core, rep = place_ref[2], place_ref[3]
-    chips, share = total.shape[0], total.shape[2]
-    height = chips * weight_ref.shape[1]
-    depth = weight_ref.shape[2]
-    block = chips * share
-    first = core == 0
-    for i in range(chunk[1]):
-        own = tile_of(own_ref, chunk[0] + i, rows.shape[2])
-        other = tile_of(other_ref, chunk[0] + i, rows.shape[2])
+def product(k, rows_ref, weight_ref, out_ref):
+    _, chips, share, depth = weight_ref.shape
+    left = weight_ref[k].reshape(chips * share, depth)
+    for start in range(0, TILES * TILE, STEP):
+        lanes = slice(start, start + STEP)
+        right = rows_ref[:, :, :, lanes].reshape(depth, STEP)
+        out_ref[:, lanes] = jnp.dot(left, right, preferred_element_type=F32).astype(out_ref.dtype)
+
+
+def join_kernel(k, place_ref, own_ref, other_ref, weight_ref, out_ref, rows_ref):
+    first = place_ref[2] == 0
+    for i in range(TILES):
+        own = tile_of(own_ref, i, rows_ref.shape[2])
+        other = tile_of(other_ref, i, rows_ref.shape[2])
         lanes = slice(i * TILE, (i + 1) * TILE)
-        rows[:, 0, :, lanes] = jnp.where(first, own, other)
-        rows[:, 1, :, lanes] = jnp.where(first, other, own)
-    step = total.shape[3]
-    for i in range(CHIPS // chips):
-        left = weight_ref[i * chips : (i + 1) * chips].reshape(height, depth)
-        here = slice(i * block, (i + 1) * block)
-        for start in range(0, rows.shape[3], step):
-            lanes = slice(start, start + step)
-            right = rows[:, :, :, lanes].reshape(depth, step)
-            term = jnp.dot(left, right, preferred_element_type=F32)
-            total[...] = term.reshape(total.shape)
-            keep_ref[here, lanes] = total[:, pl.ds(rep, 1)].reshape(block, step)
-            for shift, ref in ((1, to1_ref), (2, to2_ref), (3, to3_ref)):
-                sent = total[:, pl.ds(lax.rem(rep + shift, REPS), 1)].reshape(block, step)
-                ref[here, lanes] = sent.astype(BF16)
-
-
-def matmul(chunk, place, own, other, weights):
-    chips, height, depth = weights.shape
-    share = height // REPS
-    lanes = chunk[1] * TILE
-    shape = (CHIPS * share, lanes)
-    return pl.pallas_call(
-        functools.partial(matmul_kernel, chunk),
-        out_shape=[jax.ShapeDtypeStruct(shape, F32)] + [jax.ShapeDtypeStruct(shape, BF16)] * 3,
+        rows_ref[:, 0, :, lanes] = jnp.where(first, own, other)
+        rows_ref[:, 1, :, lanes] = jnp.where(first, other, own)
+    product(k, rows_ref, weight_ref, out_ref)
+
+
+def cost(weights):
+    _, chips, share, depth = weights.shape
+    return pl.CostEstimate(
+        flops=2 * chips * share * depth * TILES * TILE,
+        bytes_accessed=2 * chips * share * depth,
+        transcendentals=0,
+    )
+
+
+def join(k, place, own, other, weights):
+    _, chips, share, depth = weights.shape
+    rows = (chips, CORES, depth // (chips * CORES), TILES * TILE)
+    return pl.pallas_call(
+        functools.partial(join_kernel, k),
+        out_shape=[
+            jax.ShapeDtypeStruct((chips * share, TILES * TILE), BF16),
+            jax.ShapeDtypeStruct(rows, BF16),
+        ],
         in_specs=[SMEM] + [VMEM] * 3,
-        out_specs=[VMEM] * 4,
-        scratch_shapes=[
-            pltpu.VMEM((CHIPS, CORES, depth // (CHIPS * CORES), lanes), BF16),
-            pltpu.VMEM((8, REPS, share, 2 * TILE), F32),
-        ],
-        compiler_params=LIMIT,
-        cost_estimate=pl.CostEstimate(
-            flops=2 * chips * height * depth * lanes,
-            bytes_accessed=2 * chips * height * depth,
-            transcendentals=0,
-        ),
+        out_specs=[VMEM] * 2,
+        compiler_params=LIMIT,
+        cost_estimate=cost(weights),
     )(place, own, other, weights)
+
+
+def matmul(k, rows, weights):
+    _, chips, share, _ = weights.shape
+    return pl.pallas_call(
+        functools.partial(product, k),
+        out_shape=jax.ShapeDtypeStruct((chips * share, TILES * TILE), BF16 if k else F32),
+        in_specs=[VMEM] * 2,
+        out_specs=VMEM,
+        compiler_params=LIMIT,
+        cost_estimate=cost(weights),
+    )(rows, weights)
+
+
+def add_kernel(total_ref, got_ref, out_ref):
+    out_ref[...] = (total_ref[...] + got_ref[...].astype(F32)).astype(out_ref.dtype)
+
+
+def add(total, got, dtype):
+    return pl.pallas_call(
+        add_kernel,
+        out_shape=jax.ShapeDtypeStruct(total.shape, dtype),
+        in_specs=[VMEM] * 2,
+        out_specs=VMEM,
+        compiler_params=LIMIT,
+        cost_estimate=pl.CostEstimate(flops=total.size, bytes_accessed=10 * total.size, transcendentals=0),
+    )(total, got)
 
 
 def update_kernel(plan, ladder_ref, rest_ref, occupied_ref, virtual_ref, out_ref):
@@ -206,13 +229,14 @@
     return lax.optimization_barrier((array, *others))[0]
 
 
-def over_rep(chunk, place, own, other, weights):
-    keep, to1, to2, to3 = matmul(chunk, place, own, other, weights)
+def over_rep(place, own, other, weights):
+    to2, rows = join(2, place, own, other, weights)
     got2 = shifted(to2, "rep", REPS, 2)
-    got1 = shifted(to1, "rep", REPS, 1)
-    got3 = shifted(to3, "rep", REPS, 3)
-    total = keep + got1.astype(F32) + got2.astype(F32) + got3.astype(F32)
-    return total.astype(BF16)
+    got1 = shifted(matmul(1, rows, weights), "rep", REPS, 1)
+    got3 = shifted(matmul(3, rows, weights), "rep", REPS, 3)
+    total = add(matmul(0, rows, weights), got2, F32)
+    total = add(total, got1, F32)
+    return add(total, got3, BF16)
 
 
 def on_device(amplitudes, integrals, rest_terms, occupied_energy, virtual_energy, slab_start):
@@ -223,13 +247,12 @@
         occupied_energy, virtual_energy, slab_start, pair_count, share
     )
     place = jnp.stack([lax.axis_index(a) for a in ("z", "y", "core", "rep")]).astype(jnp.int32)
-    split = integrals.reshape(CHIPS, CORES, REPS * share, integrals.shape[2])
+    split = integrals.reshape(CHIPS, CORES, REPS, share, integrals.shape[2])
 
     own = lax.all_to_all(repack(plan, amp), ("z", "y"), split_axis=0, concat_axis=0, tiled=True)
     other = shifted(own, "core", CORES, 1)
     weights = hold(place, split, own)
-    totals = [over_rep(chunk, place, own, other, weights) for chunk in CHUNKS]
-    total = jnp.concatenate(totals, axis=1)
+    total = over_rep(place, own, other, weights)
     ladder = lax.all_to_all(
         total.reshape(CHIPS, share, -1), ("z", "y"), split_axis=0, concat_axis=0, tiled=True
     )

time: 125 us -> 119 us (0.952); the launches traced: 122 us -> 119 us
  starting transfers between devices: 12.8 us -> 7.63 us
  waiting for transfers between devices: 24.5 us -> 28.4 us
    ppermute x7 -> x4, starting transfers between devices: 8.97 us -> 3.75 us  [shifted(): lax.ppermute(array, axis, [(i, (i + shift) % size) for i in range(size)])]
    ppermute x7 -> x4, waiting for transfers between devices: 10.8 us -> 14 us  [shifted(): lax.ppermute(array, axis, [(i, (i + shift) % size) for i in range(size)])]
    pallas_call x3 -> x8, Pallas kernels: 12.9 us -> 11.7 us  [the longest x3 4.16 us: matmul(): pl.pallas_call(functools.partial(product, k), out_shape=jax.ShapeDtypeStr...]
  transfers between devices with their start and end apart: 8 -> 5, of which waited for: 4 -> 5; matrix products, arithmetic and copies ran while one was open for 1% -> 1% of each run, Pallas kernels for 8% -> 6%
where the time goes in v3:
time: 119 us
  blocking collectives  66.7 us (56%)
  waiting for transfers between devices  28.4 us (24%)
  Pallas kernels  13 us (11%)
  starting transfers between devices  7.63 us (6%)
  local copies, waits for them, and re-layouts  1.96 us (2%)
    all_to_all x1, blocking collectives, on_device(): lax.all_to_all(repack(plan, amp), ('z', 'y'), split_axis=0, concat_axis=0...  66.7 us
    all_to_all x1, waiting for transfers between devices, on_device(): lax.all_to_all(total.reshape(CHIPS, share, -1), ('z', 'y'), split_axis=0,...  14.4 us
    ppermute x4, waiting for transfers between devices, shifted(): lax.ppermute(array, axis, [(i, (i + shift) % size) for i in range(size)])  14 us
    pallas_call x3, Pallas kernels, matmul(): pl.pallas_call(functools.partial(product, k), out_shape=jax.ShapeDtypeStr...  4.16 us
    all_to_all x1, starting transfers between devices, on_device(): lax.all_to_all(total.reshape(CHIPS, share, -1), ('z', 'y'), split_axis=0,...  3.88 us
    ppermute x4, starting transfers between devices, shifted(): lax.ppermute(array, axis, [(i, (i + shift) % size) for i in range(size)])  3.75 us
    pallas_call x1, Pallas kernels, hold(): pl.pallas_call(hold_kernel, out_shape=jax.ShapeDtypeStruct((REPS, chips,...  3.42 us
    pallas_call x1, Pallas kernels, join(): pl.pallas_call(functools.partial(join_kernel, k), out_shape=[jax.ShapeDty...  3.21 us
  transfers between devices with their start and end apart: 5, of which 5 were waited for; matrix products, arithmetic and copies ran while one was open for 1% of the time, Pallas kernels for 6%

profile of v3, /device:TPU:6, one launch (start us, length us, event | category | flops | bytes accessed | tf_op | source)
XLA Modules:
  0.0 119.0 jit_solution(12945271237404198803)
XLA Ops:
  0.0 1.6 %copy-done = bf16[22016,1,48]{0,2,1:T(8,128)(2,1)S(1)} copy-done((bf16[22016,1,48]{0,2,1:T(8,128)(2,1)S(1)}, bf16[22016,1,48]{0,2,1:T(8,128)(2,1)}, u32[]{:S(2)}) %copy-start) | copy-done | bytes 2113560
  1.6 0.4 shard_map.64
  2.0 66.7 %all_to_all.10._.own_ref = bf16[32,272,128]{2,1,0:T(8,128)(2,1)S(1)} all-to-all(bf16[32,272,128]{2,1,0:T(8,128)(2,1)S(1)} %shard_map.64), channel_id=1, replica_groups=mesh['z'=8,'y'=4,'core'=2,'rep'=4] {'z','y'}, dimensions={0} | all-to-all | bytes 4456448 | tf_op jit(solution)/shard_map/all_to_all | solution.py:252
  68.7 0.1 pad_add_fusion.place_ref
  68.8 3.4 %shard_map.65.weight_ref = bf16[4,32,8,3072]{3,2,1,0:T(8,128)(2,1)S(1)} custom-call(s32[4]{0:T(128)S(1)} %pad_add_fusion.place_ref, bf16[32,2,4,8,3072]{4,3,2,1,0:T(8,128)(2,1)} %bitcast.15, bf16[32,272,128]{2,1,0:T(8,128)(2,1)S(1)} %all_to_all.10._.own_ref), custom_call_target="tpu_custom_call" | custom-call | tf_op jit(solution)/shard_map/pallas_call | solution.py:92
  72.2 1.0 collective-permute-done.other_ref
  73.2 3.2 %shard_map.66 = (bf16[256,768]{1,0:T(8,128)(2,1)S(1)}, bf16[32,2,48,768]{3,2,1,0:T(8,128)(2,1)S(1)}) custom-call(s32[4]{0:T(128)S(1)} %pad_add_fusion.place_ref, bf16[32,272,128]{2,1,0:T(8,128)(2,1)S(1)} %all_to_all.10._.own_ref, bf16[32,272,128]{2,1,0:T(8,128)(2,1)} %collective-permute-done.other_ref, bf16[4,32,8,3072]{3,2,1,0:T(8,128)(2,1)S(1)} %shard_map.65.weight_ref), custom_call_target="tpu_custom_call" | custom-call | flops 1207959552 | bytes 1572864 | tf_op jit(solution)/shard_map/pallas_call | solution.py:144
  76.4 1.5 %collective-permute-start.1 = (bf16[256,768]{1,0:T(8,128)(2,1)S(1)}, bf16[256,768]{1,0:T(8,128)(2,1)S(1)}, u32[]{:S(2)}, u32[]{:S(2)}) collective-permute-start(bf16[256,768]{1,0:T(8,128)(2,1)S(1)} %get-tuple-element.8), channel_id=1, source_target_pairs={{0,2},{1,3},{2,0},{3,1},{4,6},{5,7},{6,4},{7,5},{8,10},{9,11},{10,... | collective-permute-start | bytes 1179656 | tf_op jit(solution)/shard_map/ppermute | solution.py:225
  77.9 1.4 %shard_map.69 = bf16[256,768]{1,0:T(8,128)(2,1)S(1)} custom-call(bf16[32,2,48,768]{3,2,1,0:T(8,128)(2,1)S(1)} %get-tuple-element.7.rows_ref, bf16[4,32,8,3072]{3,2,1,0:T(8,128)(2,1)S(1)} %shard_map.65.weight_ref), custom_call_target="tpu_custom_call" | custom-call | flops 1207959552 | bytes 1572864 | tf_op jit(solution)/shard_map/pallas_call | solution.py:159
  79.3 2.2 %collective-permute-start.2 = (bf16[256,768]{1,0:T(8,128)(2,1)S(1)}, bf16[256,768]{1,0:T(8,128)(2,1)S(1)}, u32[]{:S(2)}, u32[]{:S(2)}) collective-permute-start(bf16[256,768]{1,0:T(8,128)(2,1)S(1)} %shard_map.69), channel_id=1, source_target_pairs={{0,1},{1,2},{2,3},{3,0},{4,5},{5,6},{6,7},{7,4},{8,9},{9,10},{10,1... | collective-permute-start | bytes 1179656 | tf_op jit(solution)/shard_map/ppermute | solution.py:225
  81.5 1.4 %shard_map.71 = bf16[256,768]{1,0:T(8,128)(2,1)S(1)} custom-call(bf16[32,2,48,768]{3,2,1,0:T(8,128)(2,1)S(1)} %get-tuple-element.7.rows_ref, bf16[4,32,8,3072]{3,2,1,0:T(8,128)(2,1)S(1)} %shard_map.65.weight_ref), custom_call_target="tpu_custom_call" | custom-call | flops 1207959552 | bytes 1572864 | tf_op jit(solution)/shard_map/pallas_call | solution.py:159
  82.9 0.1 collective-permute-start.3
  83.0 1.4 %shard_map.67.total_ref = f32[256,768]{1,0:T(8,128)S(1)} custom-call(bf16[32,2,48,768]{3,2,1,0:T(8,128)(2,1)S(1)} %get-tuple-element.7.rows_ref, bf16[4,32,8,3072]{3,2,1,0:T(8,128)(2,1)S(1)} %shard_map.65.weight_ref), custom_call_target="tpu_custom_call" | custom-call | flops 1207959552 | bytes 1572864 | tf_op jit(solution)/shard_map/pallas_call | solution.py:159
  84.3 5.6 %collective-permute-done.1.got_ref = bf16[256,768]{1,0:T(8,128)(2,1)S(1)} collective-permute-done((bf16[256,768]{1,0:T(8,128)(2,1)S(1)}, bf16[256,768]{1,0:T(8,128)(2,1)S(1)}, u32[]{:S(2)}, u32[]{:S(2)}) %collective-permute-start.1) | collective-permute-done | bytes 393248 | tf_op jit(solution)/shard_map/ppermute | solution.py:225
  90.1 5.3 %collective-permute-done.2.got_ref = bf16[256,768]{1,0:T(8,128)(2,1)S(1)} collective-permute-done((bf16[256,768]{1,0:T(8,128)(2,1)S(1)}, bf16[256,768]{1,0:T(8,128)(2,1)S(1)}, u32[]{:S(2)}, u32[]{:S(2)}) %collective-permute-start.2) | collective-permute-done | bytes 393248 | tf_op jit(solution)/shard_map/ppermute | solution.py:225
  95.5 2.1 %collective-permute-done.3.got_ref = bf16[256,768]{1,0:T(8,128)(2,1)S(1)} collective-permute-done((bf16[256,768]{1,0:T(8,128)(2,1)S(1)}, bf16[256,768]{1,0:T(8,128)(2,1)S(1)}, u32[]{:S(2)}, u32[]{:S(2)}) %collective-permute-start.3) | collective-permute-done | bytes 393248 | tf_op jit(solution)/shard_map/ppermute | solution.py:225
  97.6 0.8 shard_map.72
  98.4 3.9 %all-to-all-start.1 = ((bf16[32,8,768]{2,1,0:T(8,128)(2,1)}), bf16[32,8,768]{2,1,0:T(8,128)(2,1)S(1)}, u32[]{:S(2)}, u32[]{:S(2)}) async-start(bf16[32,8,768]{2,1,0:T(8,128)(2,1)} %bitcast.7), calls=%async_computation.1 | async-start | bytes 786432 | tf_op jit(solution)/shard_map/all_to_all | solution.py:256
  103.0 0.2 select_reduce_fusion
  103.2 0.1 copy.8.virtual_ref
  103.3 0.1 broadcast_add_fusion
  103.4 0.2 add.73
  103.7 14.4 %all-to-all-done.1.ladder_ref = bf16[32,8,768]{2,1,0:T(8,128)(2,1)S(1)} async-done(((bf16[32,8,768]{2,1,0:T(8,128)(2,1)}), bf16[32,8,768]{2,1,0:T(8,128)(2,1)S(1)}, u32[]{:S(2)}, u32[]{:S(2)}) %all-to-all-start.1) | async-done | bytes 393248 | tf_op jit(solution)/shard_map/all_to_all | solution.py:256
  118.0 0.9 shard_map.73
  (13 shorter events, 0.2 us)
Async XLA Ops:
  0.0 1.6 %copy-start = (bf16[22016,1,48]{0,2,1:T(8,128)(2,1)S(1)}, bf16[22016,1,48]{0,2,1:T(8,128)(2,1)}, u32[]{:S(2)}) copy-start(bf16[22016,1,48]{0,2,1:T(8,128)(2,1)} %param.6) | copy-start | bytes 6340612
  68.7 4.5 %collective-permute-start = (bf16[32,272,128]{2,1,0:T(8,128)(2,1)S(1)}, bf16[32,272,128]{2,1,0:T(8,128)(2,1)}, u32[]{:S(2)}, u32[]{:S(2)}) collective-permute-start(bf16[32,272,128]{2,1,0:T(8,128)(2,1)S(1)} %all_to_all.10._.own_ref), channel_id=1, source_target_pairs={{0,4},{4,0},{1,5},{5,1},{2,6},{6,2},{3,7},{7,3},{8,12},{12,8},{9,1... | collective-permute-start | bytes 6684680 | tf_op jit(solution)/shard_map/ppermute | solution.py:225
  76.4 13.6 %collective-permute-start.1 = (bf16[256,768]{1,0:T(8,128)(2,1)S(1)}, bf16[256,768]{1,0:T(8,128)(2,1)S(1)}, u32[]{:S(2)}, u32[]{:S(2)}) collective-permute-start(bf16[256,768]{1,0:T(8,128)(2,1)S(1)} %get-tuple-element.8), channel_id=1, source_target_pairs={{0,2},{1,3},{2,0},{3,1},{4,6},{5,7},{6,4},{7,5},{8,10},{9,11},{10,... | collective-permute-start | bytes 1179656 | tf_op jit(solution)/shard_map/ppermute | solution.py:225
  79.3 16.1 %collective-permute-start.2 = (bf16[256,768]{1,0:T(8,128)(2,1)S(1)}, bf16[256,768]{1,0:T(8,128)(2,1)S(1)}, u32[]{:S(2)}, u32[]{:S(2)}) collective-permute-start(bf16[256,768]{1,0:T(8,128)(2,1)S(1)} %shard_map.69), channel_id=1, source_target_pairs={{0,1},{1,2},{2,3},{3,0},{4,5},{5,6},{6,7},{7,4},{8,9},{9,10},{10,1... | collective-permute-start | bytes 1179656 | tf_op jit(solution)/shard_map/ppermute | solution.py:225
  82.9 14.7 %collective-permute-start.3 = (bf16[256,768]{1,0:T(8,128)(2,1)S(1)}, bf16[256,768]{1,0:T(8,128)(2,1)S(1)}, u32[]{:S(2)}, u32[]{:S(2)}) collective-permute-start(bf16[256,768]{1,0:T(8,128)(2,1)S(1)} %shard_map.71), channel_id=1, source_target_pairs={{0,3},{1,0},{2,1},{3,2},{4,7},{5,4},{6,5},{7,6},{8,11},{9,8},{10,9... | collective-permute-start | bytes 1179656 | tf_op jit(solution)/shard_map/ppermute | solution.py:225
  90.1 12.9 %copy-start.3 = (f32[900]{0:T(1024)S(1)}, f32[900]{0:T(1024)}, u32[]{:S(2)}) copy-start(f32[900]{0:T(1024)} %param.10) | copy-start | bytes 10804
  90.1 13.2 %copy-start.2 = (f32[150]{0:T(256)S(1)}, f32[150]{0:T(256)}, u32[]{:S(2)}) copy-start(f32[150]{0:T(256)} %param.9) | copy-start | bytes 1804
  90.1 28.0 %copy-start.1 = (bf16[8,22016]{1,0:T(8,128)(2,1)S(1)}, bf16[8,22016]{1,0:T(8,128)(2,1)}, u32[]{:S(2)}) copy-start(bf16[8,22016]{1,0:T(8,128)(2,1)} %rest_ref.1) | copy-start | bytes 1056772
  98.4 19.6 %all-to-all-start.1 = ((bf16[32,8,768]{2,1,0:T(8,128)(2,1)}), bf16[32,8,768]{2,1,0:T(8,128)(2,1)S(1)}, u32[]{:S(2)}, u32[]{:S(2)}) async-start(bf16[32,8,768]{2,1,0:T(8,128)(2,1)} %bitcast.7), calls=%async_computation.1 | async-start | bytes 786432 | tf_op jit(solution)/shard_map/all_to_all | solution.py:256

commit v4 on v3

--- a/solution.py
+++ b/solution.py
@@ -13,6 +13,8 @@
 WHOLE = 5
 TILES = WHOLE + 1
 STEP = 2 * TILE
+ORDER = (2, 1, 3)
+PIECES = (1, 1, 1, 1)
 BF16, F32 = jnp.bfloat16, jnp.float32
 ANY = pl.BlockSpec(memory_space=pl.ANY)
 VMEM = pl.BlockSpec(memory_space=pltpu.VMEM)
@@ -109,16 +111,32 @@
     return jnp.concatenate([packed.astype(BF16), swapped.astype(BF16), last], axis=1)
 
 
-def product(k, rows_ref, weight_ref, out_ref):
+def product(k, rows_ref, weight_ref, outs):
     _, chips, share, depth = weight_ref.shape
-    left = weight_ref[k].reshape(chips * share, depth)
+    height = chips * share
+    left = weight_ref[k].reshape(height, depth)
+    parts = []
     for start in range(0, TILES * TILE, STEP):
-        lanes = slice(start, start + STEP)
-        right = rows_ref[:, :, :, lanes].reshape(depth, STEP)
-        out_ref[:, lanes] = jnp.dot(left, right, preferred_element_type=F32).astype(out_ref.dtype)
-
-
-def join_kernel(k, place_ref, own_ref, other_ref, weight_ref, out_ref, rows_ref):
+        right = rows_ref[:, :, :, start : start + STEP].reshape(depth, STEP)
+        term = jnp.dot(left, right, preferred_element_type=F32)
+        parts += [term[:, :TILE], term[:, TILE:]]
+    low = lax.broadcasted_iota(jnp.int32, (height // 2, TILE), 1) < HALF
+    last = parts.pop()
+    parts.append(jnp.where(low, last[: height // 2], swap_halves(last[height // 2 :])))
+    at, end = 0, outs[0].shape[0]
+    place = 0
+    for part in parts:
+        part = part.astype(outs[0].dtype)
+        done = 0
+        while done < part.shape[0]:
+            size = min(part.shape[0] - done, end - at)
+            outs[place][at : at + size] = part[done : done + size]
+            at, done = at + size, done + size
+            if at == end:
+                place, at = place + 1, 0
+
+
+def join_kernel(k, place_ref, own_ref, other_ref, weight_ref, rows_ref, *outs):
     first = place_ref[2] == 0
     for i in range(TILES):
         own = tile_of(own_ref, i, rows_ref.shape[2])
@@ -126,7 +144,7 @@
         lanes = slice(i * TILE, (i + 1) * TILE)
         rows_ref[:, 0, :, lanes] = jnp.where(first, own, other)
         rows_ref[:, 1, :, lanes] = jnp.where(first, other, own)
-    product(k, rows_ref, weight_ref, out_ref)
+    product(k, rows_ref, weight_ref, outs)
 
 
 def cost(weights):
@@ -138,47 +156,73 @@
     )
 
 
+def packed(weights, pieces, dtype):
+    height = weights.shape[1] * weights.shape[2]
+    return [jax.ShapeDtypeStruct(((2 * WHOLE + 1) * height // 2 // pieces, TILE), dtype)] * pieces
+
+
 def join(k, place, own, other, weights):
-    _, chips, share, depth = weights.shape
+    _, chips, _, depth = weights.shape
     rows = (chips, CORES, depth // (chips * CORES), TILES * TILE)
-    return pl.pallas_call(
+    rows, *outs = pl.pallas_call(
         functools.partial(join_kernel, k),
-        out_shape=[
-            jax.ShapeDtypeStruct((chips * share, TILES * TILE), BF16),
-            jax.ShapeDtypeStruct(rows, BF16),
-        ],
+        out_shape=[jax.ShapeDtypeStruct(rows, BF16)] + packed(weights, PIECES[k], BF16),
         in_specs=[SMEM] + [VMEM] * 3,
-        out_specs=[VMEM] * 2,
+        out_specs=[VMEM] * (1 + PIECES[k]),
         compiler_params=LIMIT,
         cost_estimate=cost(weights),
     )(place, own, other, weights)
+    return outs, rows
+
+
+def matmul_kernel(k, rows_ref, weight_ref, *outs):
+    product(k, rows_ref, weight_ref, outs)
 
 
 def matmul(k, rows, weights):
-    _, chips, share, _ = weights.shape
-    return pl.pallas_call(
-        functools.partial(product, k),
-        out_shape=jax.ShapeDtypeStruct((chips * share, TILES * TILE), BF16 if k else F32),
+    return pl.pallas_call(
+        functools.partial(matmul_kernel, k),
+        out_shape=packed(weights, PIECES[k], BF16 if k else F32),
         in_specs=[VMEM] * 2,
-        out_specs=VMEM,
+        out_specs=[VMEM] * PIECES[k],
         compiler_params=LIMIT,
         cost_estimate=cost(weights),
     )(rows, weights)
 
 
-def add_kernel(total_ref, got_ref, out_ref):
-    out_ref[...] = (total_ref[...] + got_ref[...].astype(F32)).astype(out_ref.dtype)
-
-
-def add(total, got, dtype):
-    return pl.pallas_call(
-        add_kernel,
-        out_shape=jax.ShapeDtypeStruct(total.shape, dtype),
-        in_specs=[VMEM] * 2,
+def add_kernel(total_ref, *refs):
+    gots, out_ref = refs[:-1], refs[-1]
+    size = gots[0].shape[0]
+    for i, got in enumerate(gots):
+        here = slice(i * size, (i + 1) * size)
+        out_ref[here] = total_ref[here] + got[...].astype(F32)
+
+
+def add_last_kernel(total_ref, *refs):
+    gots, out_ref = refs[:-1], refs[-1]
+    size, height = gots[0].shape[0], out_ref.shape[0]
+    whole = jnp.concatenate([got[...].astype(F32) for got in gots], axis=0) + total_ref[...]
+    for place in range(WHOLE):
+        part = whole[place * height : (place + 1) * height]
+        out_ref[:, place * TILE : (place + 1) * TILE] = part.astype(BF16)
+    part = whole[WHOLE * height :]
+    part = jnp.concatenate([part, swap_halves(part)], axis=0)
+    out_ref[:, WHOLE * TILE :] = part.astype(BF16)
+
+
+def add(total, gots, last=False):
+    height = 2 * total.shape[0] // (2 * WHOLE + 1)
+    shape = jax.ShapeDtypeStruct((height, TILES * TILE), BF16)
+    return pl.pallas_call(
+        add_last_kernel if last else add_kernel,
+        out_shape=shape if last else jax.ShapeDtypeStruct(total.shape, F32),
+        in_specs=[VMEM] * (1 + len(gots)),
         out_specs=VMEM,
         compiler_params=LIMIT,
-        cost_estimate=pl.CostEstimate(flops=total.size, bytes_accessed=10 * total.size, transcendentals=0),
-    )(total, got)
+        cost_estimate=pl.CostEstimate(
+            flops=total.size, bytes_accessed=10 * total.size, transcendentals=0
+        ),
+    )(total, *gots)
 
 
 def update_kernel(plan, ladder_ref, rest_ref, occupied_ref, virtual_ref, out_ref):
@@ -230,13 +274,15 @@
 
 
 def over_rep(place, own, other, weights):
-    to2, rows = join(2, place, own, other, weights)
-    got2 = shifted(to2, "rep", REPS, 2)
-    got1 = shifted(matmul(1, rows, weights), "rep", REPS, 1)
-    got3 = shifted(matmul(3, rows, weights), "rep", REPS, 3)
-    total = add(matmul(0, rows, weights), got2, F32)
-    total = add(total, got1, F32)
-    return add(total, got3, BF16)
+    sent, rows = join(ORDER[0], place, own, other, weights)
+    got = []
+    for k in ORDER:
+        blocks = sent if k == ORDER[0] else matmul(k, rows, weights)
+        got.append([shifted(block, "rep", REPS, k) for block in blocks])
+    total = matmul(0, rows, weights)[0]
+    for blocks in got[:-1]:
+        total = add(total, blocks)
+    return add(total, got[-1], last=True)
 
 
 def on_device(amplitudes, integrals, rest_terms, occupied_energy, virtual_energy, slab_start):

time: 119 us -> 118 us (level)
  waiting for transfers between devices: 28.4 us -> 26.8 us
    ppermute x4, waiting for transfers between devices: 14 us -> 12.4 us  [shifted(): lax.ppermute(array, axis, [(i, (i + shift) % size) for i in range(size)])]
  transfers between devices with their start and end apart: 5 -> 5, of which waited for: 5 -> 5; matrix products, arithmetic and copies ran while one was open for 1% -> 1% of each run, Pallas kernels for 6% -> 7%
where the time goes in v4:
time: 118 us
  blocking collectives  66.7 us (57%)
  waiting for transfers between devices  26.8 us (23%)
  Pallas kernels  13.4 us (11%)
  starting transfers between devices  7.63 us (6%)
  local copies, waits for them, and re-layouts  1.96 us (2%)
    all_to_all x1, blocking collectives, on_device(): lax.all_to_all(repack(plan, amp), ('z', 'y'), split_axis=0, concat_axis=0...  66.7 us
    all_to_all x1, waiting for transfers between devices, on_device(): lax.all_to_all(total.reshape(CHIPS, share, -1), ('z', 'y'), split_axis=0,...  14.4 us
    ppermute x4, waiting for transfers between devices, shifted(): lax.ppermute(array, axis, [(i, (i + shift) % size) for i in range(size)])  12.4 us
    pallas_call x3, Pallas kernels, matmul(): pl.pallas_call(functools.partial(matmul_kernel, k), out_shape=packed(weig...  4.38 us
    all_to_all x1, starting transfers between devices, on_device(): lax.all_to_all(total.reshape(CHIPS, share, -1), ('z', 'y'), split_axis=0,...  3.88 us
    ppermute x4, starting transfers between devices, shifted(): lax.ppermute(array, axis, [(i, (i + shift) % size) for i in range(size)])  3.75 us
    pallas_call x1, Pallas kernels, hold(): pl.pallas_call(hold_kernel, out_shape=jax.ShapeDtypeStruct((REPS, chips,...  3.42 us
    pallas_call x1, Pallas kernels, join(): pl.pallas_call(functools.partial(join_kernel, k), out_shape=[jax.ShapeDty...  3.28 us
  transfers between devices with their start and end apart: 5, of which 5 were waited for; matrix products, arithmetic and copies ran while one was open for 1% of the time, Pallas kernels for 7%

profile of v4, /device:TPU:6, one launch (start us, length us, event | category | flops | bytes accessed | tf_op | source)
XLA Modules:
  0.0 117.7 jit_solution(9197874022824908827)
XLA Ops:
  0.0 1.6 %copy-done = bf16[22016,1,48]{0,2,1:T(8,128)(2,1)S(1)} copy-done((bf16[22016,1,48]{0,2,1:T(8,128)(2,1)S(1)}, bf16[22016,1,48]{0,2,1:T(8,128)(2,1)}, u32[]{:S(2)}) %copy-start) | copy-done | bytes 2113560
  1.6 0.4 shard_map.64
  2.0 66.7 %all_to_all.10._.own_ref = bf16[32,272,128]{2,1,0:T(8,128)(2,1)S(1)} all-to-all(bf16[32,272,128]{2,1,0:T(8,128)(2,1)S(1)} %shard_map.64), channel_id=1, replica_groups=mesh['z'=8,'y'=4,'core'=2,'rep'=4] {'z','y'}, dimensions={0} | all-to-all | bytes 4456448 | tf_op jit(solution)/shard_map/all_to_all | solution.py:298
  68.7 0.1 pad_add_fusion.place_ref
  68.8 3.4 %shard_map.65.weight_ref = bf16[4,32,8,3072]{3,2,1,0:T(8,128)(2,1)S(1)} custom-call(s32[4]{0:T(128)S(1)} %pad_add_fusion.place_ref, bf16[32,2,4,8,3072]{4,3,2,1,0:T(8,128)(2,1)} %bitcast.15, bf16[32,272,128]{2,1,0:T(8,128)(2,1)S(1)} %all_to_all.10._.own_ref), custom_call_target="tpu_custom_call" | custom-call | tf_op jit(solution)/shard_map/pallas_call | solution.py:94
  72.2 1.0 collective-permute-done.other_ref
  73.2 3.3 %shard_map.66 = (bf16[32,2,48,768]{3,2,1,0:T(8,128)(2,1)S(1)}, bf16[1408,128]{1,0:T(8,128)(2,1)S(1)}) custom-call(s32[4]{0:T(128)S(1)} %pad_add_fusion.place_ref, bf16[32,272,128]{2,1,0:T(8,128)(2,1)S(1)} %all_to_all.10._.own_ref, bf16[32,272,128]{2,1,0:T(8,128)(2,1)} %collective-permute-done.other_ref, bf16[4,32,8,3072]{3,2,1,0:T(8,128)(2,1)S(1)} %shard_map.65.weight_ref), custom_call_target="tpu_custom_call" | custom-call | flops 1207959552 | bytes 1572864 | tf_op jit(solution)/shard_map/pallas_call | solution.py:167
  76.5 1.5 %collective-permute-start.1 = (bf16[1408,128]{1,0:T(8,128)(2,1)S(1)}, bf16[1408,128]{1,0:T(8,128)(2,1)S(1)}, u32[]{:S(2)}, u32[]{:S(2)}) collective-permute-start(bf16[1408,128]{1,0:T(8,128)(2,1)S(1)} %get-tuple-element.8), channel_id=1, source_target_pairs={{0,2},{1,3},{2,0},{3,1},{4,6},{5,7},{6,4},{7,5},{8,10},{9,11},{10,... | collective-permute-start | bytes 1081352 | tf_op jit(solution)/shard_map/ppermute | solution.py:269
  78.0 1.5 %shard_map.69 = bf16[1408,128]{1,0:T(8,128)(2,1)S(1)} custom-call(bf16[32,2,48,768]{3,2,1,0:T(8,128)(2,1)S(1)} %get-tuple-element.7.rows_ref, bf16[4,32,8,3072]{3,2,1,0:T(8,128)(2,1)S(1)} %shard_map.65.weight_ref), custom_call_target="tpu_custom_call" | custom-call | flops 1207959552 | bytes 1572864 | tf_op jit(solution)/shard_map/pallas_call | solution.py:183
  79.4 2.2 %collective-permute-start.2 = (bf16[1408,128]{1,0:T(8,128)(2,1)S(1)}, bf16[1408,128]{1,0:T(8,128)(2,1)S(1)}, u32[]{:S(2)}, u32[]{:S(2)}) collective-permute-start(bf16[1408,128]{1,0:T(8,128)(2,1)S(1)} %shard_map.69), channel_id=1, source_target_pairs={{0,1},{1,2},{2,3},{3,0},{4,5},{5,6},{6,7},{7,4},{8,9},{9,10},{10,1... | collective-permute-start | bytes 1081352 | tf_op jit(solution)/shard_map/ppermute | solution.py:269
  81.6 1.5 %shard_map.71 = bf16[1408,128]{1,0:T(8,128)(2,1)S(1)} custom-call(bf16[32,2,48,768]{3,2,1,0:T(8,128)(2,1)S(1)} %get-tuple-element.7.rows_ref, bf16[4,32,8,3072]{3,2,1,0:T(8,128)(2,1)S(1)} %shard_map.65.weight_ref), custom_call_target="tpu_custom_call" | custom-call | flops 1207959552 | bytes 1572864 | tf_op jit(solution)/shard_map/pallas_call | solution.py:183
  83.1 0.1 collective-permute-start.3
  83.2 1.5 %shard_map.67.total_ref = f32[1408,128]{1,0:T(8,128)S(1)} custom-call(bf16[32,2,48,768]{3,2,1,0:T(8,128)(2,1)S(1)} %get-tuple-element.7.rows_ref, bf16[4,32,8,3072]{3,2,1,0:T(8,128)(2,1)S(1)} %shard_map.65.weight_ref), custom_call_target="tpu_custom_call" | custom-call | flops 1207959552 | bytes 1572864 | tf_op jit(solution)/shard_map/pallas_call | solution.py:183
  84.6 4.7 %collective-permute-done.1.refs_0_ = bf16[1408,128]{1,0:T(8,128)(2,1)S(1)} collective-permute-done((bf16[1408,128]{1,0:T(8,128)(2,1)S(1)}, bf16[1408,128]{1,0:T(8,128)(2,1)S(1)}, u32[]{:S(2)}, u32[]{:S(2)}) %collective-permute-start.1) | collective-permute-done | bytes 360480 | tf_op jit(solution)/shard_map/ppermute | solution.py:269
  89.4 4.7 %collective-permute-done.2.refs_0_ = bf16[1408,128]{1,0:T(8,128)(2,1)S(1)} collective-permute-done((bf16[1408,128]{1,0:T(8,128)(2,1)S(1)}, bf16[1408,128]{1,0:T(8,128)(2,1)S(1)}, u32[]{:S(2)}, u32[]{:S(2)}) %collective-permute-start.2) | collective-permute-done | bytes 360480 | tf_op jit(solution)/shard_map/ppermute | solution.py:269
  94.2 2.1 %collective-permute-done.3.refs_0_ = bf16[1408,128]{1,0:T(8,128)(2,1)S(1)} collective-permute-done((bf16[1408,128]{1,0:T(8,128)(2,1)S(1)}, bf16[1408,128]{1,0:T(8,128)(2,1)S(1)}, u32[]{:S(2)}, u32[]{:S(2)}) %collective-permute-start.3) | collective-permute-done | bytes 360480 | tf_op jit(solution)/shard_map/ppermute | solution.py:269
  96.2 0.9 shard_map.72
  97.1 3.9 %all-to-all-start.1 = ((bf16[32,8,768]{2,1,0:T(8,128)(2,1)}), bf16[32,8,768]{2,1,0:T(8,128)(2,1)S(1)}, u32[]{:S(2)}, u32[]{:S(2)}) async-start(bf16[32,8,768]{2,1,0:T(8,128)(2,1)} %bitcast.7), calls=%async_computation.1 | async-start | bytes 786432 | tf_op jit(solution)/shard_map/all_to_all | solution.py:302
  101.7 0.2 select_reduce_fusion
  101.9 0.1 copy.8.virtual_ref
  102.0 0.1 broadcast_add_fusion
  102.1 0.2 add.73
  102.4 14.4 %all-to-all-done.1.ladder_ref = bf16[32,8,768]{2,1,0:T(8,128)(2,1)S(1)} async-done(((bf16[32,8,768]{2,1,0:T(8,128)(2,1)}), bf16[32,8,768]{2,1,0:T(8,128)(2,1)S(1)}, u32[]{:S(2)}, u32[]{:S(2)}) %all-to-all-start.1) | async-done | bytes 393248 | tf_op jit(solution)/shard_map/all_to_all | solution.py:302
  116.8 0.9 shard_map.73
  (13 shorter events, 0.2 us)
Async XLA Ops:
  0.0 1.6 %copy-start = (bf16[22016,1,48]{0,2,1:T(8,128)(2,1)S(1)}, bf16[22016,1,48]{0,2,1:T(8,128)(2,1)}, u32[]{:S(2)}) copy-start(bf16[22016,1,48]{0,2,1:T(8,128)(2,1)} %param.6) | copy-start | bytes 6340612
  68.7 4.5 %collective-permute-start = (bf16[32,272,128]{2,1,0:T(8,128)(2,1)S(1)}, bf16[32,272,128]{2,1,0:T(8,128)(2,1)}, u32[]{:S(2)}, u32[]{:S(2)}) collective-permute-start(bf16[32,272,128]{2,1,0:T(8,128)(2,1)S(1)} %all_to_all.10._.own_ref), channel_id=1, source_target_pairs={{0,4},{4,0},{1,5},{5,1},{2,6},{6,2},{3,7},{7,3},{8,12},{12,8},{9,1... | collective-permute-start | bytes 6684680 | tf_op jit(solution)/shard_map/ppermute | solution.py:269
  76.5 12.8 %collective-permute-start.1 = (bf16[1408,128]{1,0:T(8,128)(2,1)S(1)}, bf16[1408,128]{1,0:T(8,128)(2,1)S(1)}, u32[]{:S(2)}, u32[]{:S(2)}) collective-permute-start(bf16[1408,128]{1,0:T(8,128)(2,1)S(1)} %get-tuple-element.8), channel_id=1, source_target_pairs={{0,2},{1,3},{2,0},{3,1},{4,6},{5,7},{6,4},{7,5},{8,10},{9,11},{10,... | collective-permute-start | bytes 1081352 | tf_op jit(solution)/shard_map/ppermute | solution.py:269
  79.4 14.7 %collective-permute-start.2 = (bf16[1408,128]{1,0:T(8,128)(2,1)S(1)}, bf16[1408,128]{1,0:T(8,128)(2,1)S(1)}, u32[]{:S(2)}, u32[]{:S(2)}) collective-permute-start(bf16[1408,128]{1,0:T(8,128)(2,1)S(1)} %shard_map.69), channel_id=1, source_target_pairs={{0,1},{1,2},{2,3},{3,0},{4,5},{5,6},{6,7},{7,4},{8,9},{9,10},{10,1... | collective-permute-start | bytes 1081352 | tf_op jit(solution)/shard_map/ppermute | solution.py:269
  83.1 13.2 %collective-permute-start.3 = (bf16[1408,128]{1,0:T(8,128)(2,1)S(1)}, bf16[1408,128]{1,0:T(8,128)(2,1)S(1)}, u32[]{:S(2)}, u32[]{:S(2)}) collective-permute-start(bf16[1408,128]{1,0:T(8,128)(2,1)S(1)} %shard_map.71), channel_id=1, source_target_pairs={{0,3},{1,0},{2,1},{3,2},{4,7},{5,4},{6,5},{7,6},{8,11},{9,8},{10,9... | collective-permute-start | bytes 1081352 | tf_op jit(solution)/shard_map/ppermute | solution.py:269
  89.4 12.3 %copy-start.3 = (f32[900]{0:T(1024)S(1)}, f32[900]{0:T(1024)}, u32[]{:S(2)}) copy-start(f32[900]{0:T(1024)} %param.10) | copy-start | bytes 10804
  89.4 12.6 %copy-start.2 = (f32[150]{0:T(256)S(1)}, f32[150]{0:T(256)}, u32[]{:S(2)}) copy-start(f32[150]{0:T(256)} %param.9) | copy-start | bytes 1804
  89.4 27.4 %copy-start.1 = (bf16[8,22016]{1,0:T(8,128)(2,1)S(1)}, bf16[8,22016]{1,0:T(8,128)(2,1)}, u32[]{:S(2)}) copy-start(bf16[8,22016]{1,0:T(8,128)(2,1)} %rest_ref.1) | copy-start | bytes 1056772
  97.1 19.6 %all-to-all-start.1 = ((bf16[32,8,768]{2,1,0:T(8,128)(2,1)}), bf16[32,8,768]{2,1,0:T(8,128)(2,1)S(1)}, u32[]{:S(2)}, u32[]{:S(2)}) async-start(bf16[32,8,768]{2,1,0:T(8,128)(2,1)} %bitcast.7), calls=%async_computation.1 | async-start | bytes 786432 | tf_op jit(solution)/shard_map/all_to_all | solution.py:302

commit v5 on v4

--- a/solution.py
+++ b/solution.py
@@ -13,7 +13,7 @@
 WHOLE = 5
 TILES = WHOLE + 1
 STEP = 2 * TILE
-ORDER = (2, 1, 3)
+ORDER = (1, 2, 3)
 PIECES = (1, 1, 1, 1)
 BF16, F32 = jnp.bfloat16, jnp.float32
 ANY = pl.BlockSpec(memory_space=pl.ANY)
@@ -49,8 +49,8 @@
 
 def repack_kernel(plan, amp_ref, out_ref):
     depth = amp_ref.shape[0]
-    third = depth // 3
-    low = lax.broadcasted_iota(jnp.int32, (third, TILE), 1) < HALF
+    middle = depth // 2
+    low = lax.broadcasted_iota(jnp.int32, (middle, TILE), 1) < HALF
     for h in range(CHIPS):
         for place in range(WHOLE):
             start = (plan.first[h] + place) * TILE
@@ -59,16 +59,15 @@
         other = swap_halves(block)
         if plan.odd[h]:
             block, other = other, block
-        packed = jnp.where(low, block[:third], other[third : 2 * third])
-        out_ref[h, WHOLE * depth : WHOLE * depth + third] = packed.astype(BF16)
-        out_ref[h, WHOLE * depth + third : WHOLE * depth + 2 * third] = block[2 * third :].astype(BF16)
+        packed = jnp.where(low, block[:middle], other[middle:])
+        out_ref[h, WHOLE * depth :] = packed.astype(BF16)
 
 
 def repack(plan, amp):
     depth = amp.shape[0]
     return pl.pallas_call(
         functools.partial(repack_kernel, plan),
-        out_shape=jax.ShapeDtypeStruct((CHIPS, WHOLE * depth + 2 * depth // 3, TILE), BF16),
+        out_shape=jax.ShapeDtypeStruct((CHIPS, WHOLE * depth + depth // 2, TILE), BF16),
         in_specs=[VMEM],
         out_specs=VMEM,
         compiler_params=LIMIT,
@@ -104,11 +103,9 @@
 def tile_of(ref, place, depth):
     if place < WHOLE:
         return ref[:, place * depth : (place + 1) * depth]
-    third = depth // 3
-    packed = ref[:, WHOLE * depth : WHOLE * depth + third].astype(F32)
+    packed = ref[:, WHOLE * depth :].astype(F32)
     swapped = jnp.concatenate([packed[:, :, HALF:], packed[:, :, :HALF]], axis=2)
-    last = ref[:, WHOLE * depth + third : WHOLE * depth + 2 * third]
-    return jnp.concatenate([packed.astype(BF16), swapped.astype(BF16), last], axis=1)
+    return jnp.concatenate([packed, swapped], axis=1).astype(BF16)
 
 
 def product(k, rows_ref, weight_ref, outs):
@@ -295,7 +292,8 @@
     place = jnp.stack([lax.axis_index(a) for a in ("z", "y", "core", "rep")]).astype(jnp.int32)
     split = integrals.reshape(CHIPS, CORES, REPS, share, integrals.shape[2])
 
-    own = lax.all_to_all(repack(plan, amp), ("z", "y"), split_axis=0, concat_axis=0, tiled=True)
+    sent, place = lax.optimization_barrier((repack(plan, amp), place))
+    own = lax.all_to_all(sent, ("z", "y"), split_axis=0, concat_axis=0, tiled=True)
     other = shifted(own, "core", CORES, 1)
     weights = hold(place, split, own)
     total = over_rep(place, own, other, weights)

time: 118 us -> 117 us (level)
  waiting for transfers between devices: 26.8 us -> 28.2 us
  blocking collectives: 66.7 us -> 65.5 us
    ppermute x4, waiting for transfers between devices: 12.4 us -> 13.8 us  [shifted(): lax.ppermute(array, axis, [(i, (i + shift) % size) for i in range(size)])]
    all_to_all x1, blocking collectives: 66.7 us -> 65.5 us  [on_device(): lax.all_to_all(sent, ('z', 'y'), split_axis=0, concat_axis=0, tiled=True)]
  transfers between devices with their start and end apart: 5 -> 5, of which waited for: 5 -> 4; matrix products, arithmetic and copies ran while one was open for 1% -> 1% of each run, Pallas kernels for 7% -> 6%
where the time goes in v5:
time: 117 us
  blocking collectives  65.5 us (56%)
  waiting for transfers between devices  28.2 us (24%)
  Pallas kernels  12.3 us (11%)
  starting transfers between devices  7.55 us (6%)
  local copies, waits for them, and re-layouts  1.96 us (2%)
    all_to_all x1, blocking collectives, on_device(): lax.all_to_all(sent, ('z', 'y'), split_axis=0, concat_axis=0, tiled=True)  65.5 us
    all_to_all x1, waiting for transfers between devices, on_device(): lax.all_to_all(total.reshape(CHIPS, share, -1), ('z', 'y'), split_axis=0,...  14.4 us
    ppermute x4, waiting for transfers between devices, shifted(): lax.ppermute(array, axis, [(i, (i + shift) % size) for i in range(size)])  13.8 us
    pallas_call x3, Pallas kernels, matmul(): pl.pallas_call(functools.partial(matmul_kernel, k), out_shape=packed(weig...  4.38 us
    all_to_all x1, starting transfers between devices, on_device(): lax.all_to_all(total.reshape(CHIPS, share, -1), ('z', 'y'), split_axis=0,...  3.88 us
    ppermute x4, starting transfers between devices, shifted(): lax.ppermute(array, axis, [(i, (i + shift) % size) for i in range(size)])  3.67 us
    pallas_call x1, Pallas kernels, hold(): pl.pallas_call(hold_kernel, out_shape=jax.ShapeDtypeStruct((REPS, chips,...  3.42 us
  transfers between devices with their start and end apart: 5, of which 4 were waited for; matrix products, arithmetic and copies ran while one was open for 1% of the time, Pallas kernels for 6%

profile of v5, /device:TPU:6, one launch (start us, length us, event | category | flops | bytes accessed | tf_op | source)
XLA Modules:
  0.0 116.7 jit_solution(17329871039170709333)
XLA Ops:
  0.0 1.6 %copy-done = bf16[22016,1,48]{0,2,1:T(8,128)(2,1)S(1)} copy-done((bf16[22016,1,48]{0,2,1:T(8,128)(2,1)S(1)}, bf16[22016,1,48]{0,2,1:T(8,128)(2,1)}, u32[]{:S(2)}) %copy-start) | copy-done | bytes 2113560
  1.6 0.4 shard_map.64
  2.0 0.1 pad_add_fusion.place_ref
  2.1 65.5 %all_to_all.10._.own_ref = bf16[32,264,128]{2,1,0:T(8,128)(2,1)S(1)} all-to-all(bf16[32,264,128]{2,1,0:T(8,128)(2,1)S(1)} %shard_map.64), channel_id=1, replica_groups=mesh['z'=8,'y'=4,'core'=2,'rep'=4] {'z','y'}, dimensions={0} | all-to-all | bytes 4325376 | tf_op jit(solution)/shard_map/all_to_all | solution.py:296
  67.5 3.4 %shard_map.65.weight_ref = bf16[4,32,8,3072]{3,2,1,0:T(8,128)(2,1)S(1)} custom-call(s32[4]{0:T(128)S(1)} %pad_add_fusion.place_ref, bf16[32,2,4,8,3072]{4,3,2,1,0:T(8,128)(2,1)} %bitcast.15, bf16[32,264,128]{2,1,0:T(8,128)(2,1)S(1)} %all_to_all.10._.own_ref), custom_call_target="tpu_custom_call" | custom-call | tf_op jit(solution)/shard_map/pallas_call | solution.py:93
  71.0 0.8 collective-permute-done.other_ref
  71.8 2.2 %shard_map.66 = (bf16[32,2,48,768]{3,2,1,0:T(8,128)(2,1)S(1)}, bf16[1408,128]{1,0:T(8,128)(2,1)S(1)}) custom-call(s32[4]{0:T(128)S(1)} %pad_add_fusion.place_ref, bf16[32,264,128]{2,1,0:T(8,128)(2,1)S(1)} %all_to_all.10._.own_ref, bf16[32,264,128]{2,1,0:T(8,128)(2,1)S(1)} %collective-permute-done.other_ref, bf16[4,32,8,3072]{3,2,1,0:T(8,128)(2,1)S(1)} %shard_map.65.weight_ref), custom_call_target="tpu_custom_call" | custom-call | flops 1207959552 | bytes 1572864 | tf_op jit(solution)/shard_map/pallas_call | solution.py:164
  74.0 1.5 %shard_map.69 = bf16[1408,128]{1,0:T(8,128)(2,1)S(1)} custom-call(bf16[32,2,48,768]{3,2,1,0:T(8,128)(2,1)S(1)} %get-tuple-element.11.rows_ref, bf16[4,32,8,3072]{3,2,1,0:T(8,128)(2,1)S(1)} %shard_map.65.weight_ref), custom_call_target="tpu_custom_call" | custom-call | flops 1207959552 | bytes 1572864 | tf_op jit(solution)/shard_map/pallas_call | solution.py:180
  75.4 1.5 %collective-permute-start.2 = (bf16[1408,128]{1,0:T(8,128)(2,1)S(1)}, bf16[1408,128]{1,0:T(8,128)(2,1)S(1)}, u32[]{:S(2)}, u32[]{:S(2)}) collective-permute-start(bf16[1408,128]{1,0:T(8,128)(2,1)S(1)} %shard_map.69), channel_id=1, source_target_pairs={{0,2},{1,3},{2,0},{3,1},{4,6},{5,7},{6,4},{7,5},{8,10},{9,11},{10,... | collective-permute-start | bytes 1081352 | tf_op jit(solution)/shard_map/ppermute | solution.py:266
  76.9 2.1 %collective-permute-start.1 = (bf16[1408,128]{1,0:T(8,128)(2,1)S(1)}, bf16[1408,128]{1,0:T(8,128)(2,1)S(1)}, u32[]{:S(2)}, u32[]{:S(2)}) collective-permute-start(bf16[1408,128]{1,0:T(8,128)(2,1)S(1)} %get-tuple-element.12), channel_id=1, source_target_pairs={{0,1},{1,2},{2,3},{3,0},{4,5},{5,6},{6,7},{7,4},{8,9},{9,10},{10,1... | collective-permute-start | bytes 1081352 | tf_op jit(solution)/shard_map/ppermute | solution.py:266
  79.0 1.5 %shard_map.71 = bf16[1408,128]{1,0:T(8,128)(2,1)S(1)} custom-call(bf16[32,2,48,768]{3,2,1,0:T(8,128)(2,1)S(1)} %get-tuple-element.11.rows_ref, bf16[4,32,8,3072]{3,2,1,0:T(8,128)(2,1)S(1)} %shard_map.65.weight_ref), custom_call_target="tpu_custom_call" | custom-call | flops 1207959552 | bytes 1572864 | tf_op jit(solution)/shard_map/pallas_call | solution.py:180
  80.5 0.1 collective-permute-start.3
  80.6 1.5 %shard_map.67.total_ref = f32[1408,128]{1,0:T(8,128)S(1)} custom-call(bf16[32,2,48,768]{3,2,1,0:T(8,128)(2,1)S(1)} %get-tuple-element.11.rows_ref, bf16[4,32,8,3072]{3,2,1,0:T(8,128)(2,1)S(1)} %shard_map.65.weight_ref), custom_call_target="tpu_custom_call" | custom-call | flops 1207959552 | bytes 1572864 | tf_op jit(solution)/shard_map/pallas_call | solution.py:180
  82.0 11.0 %collective-permute-done.1.refs_0_ = bf16[1408,128]{1,0:T(8,128)(2,1)S(1)} collective-permute-done((bf16[1408,128]{1,0:T(8,128)(2,1)S(1)}, bf16[1408,128]{1,0:T(8,128)(2,1)S(1)}, u32[]{:S(2)}, u32[]{:S(2)}) %collective-permute-start.1) | collective-permute-done | bytes 360480 | tf_op jit(solution)/shard_map/ppermute | solution.py:266
  93.2 2.0 %collective-permute-done.3.refs_0_ = bf16[1408,128]{1,0:T(8,128)(2,1)S(1)} collective-permute-done((bf16[1408,128]{1,0:T(8,128)(2,1)S(1)}, bf16[1408,128]{1,0:T(8,128)(2,1)S(1)}, u32[]{:S(2)}, u32[]{:S(2)}) %collective-permute-start.3) | collective-permute-done | bytes 360480 | tf_op jit(solution)/shard_map/ppermute | solution.py:266
  95.2 0.9 shard_map.72
  96.1 3.9 %all-to-all-start.1 = ((bf16[32,8,768]{2,1,0:T(8,128)(2,1)}), bf16[32,8,768]{2,1,0:T(8,128)(2,1)S(1)}, u32[]{:S(2)}, u32[]{:S(2)}) async-start(bf16[32,8,768]{2,1,0:T(8,128)(2,1)} %bitcast.7), calls=%async_computation.1 | async-start | bytes 786432 | tf_op jit(solution)/shard_map/all_to_all | solution.py:300
  100.7 0.2 select_reduce_fusion
  100.9 0.1 copy.8.virtual_ref
  101.0 0.1 broadcast_add_fusion
  101.1 0.2 add.73
  101.3 0.1 broadcast_in_dim.28.occupied_ref
  101.3 14.4 %all-to-all-done.1.ladder_ref = bf16[32,8,768]{2,1,0:T(8,128)(2,1)S(1)} async-done(((bf16[32,8,768]{2,1,0:T(8,128)(2,1)}), bf16[32,8,768]{2,1,0:T(8,128)(2,1)S(1)}, u32[]{:S(2)}, u32[]{:S(2)}) %all-to-all-start.1) | async-done | bytes 393248 | tf_op jit(solution)/shard_map/all_to_all | solution.py:300
  115.7 0.9 shard_map.73
  (13 shorter events, 0.2 us)
Async XLA Ops:
  0.0 1.6 %copy-start = (bf16[22016,1,48]{0,2,1:T(8,128)(2,1)S(1)}, bf16[22016,1,48]{0,2,1:T(8,128)(2,1)}, u32[]{:S(2)}) copy-start(bf16[22016,1,48]{0,2,1:T(8,128)(2,1)} %param.6) | copy-start | bytes 6340612
  67.5 4.3 %collective-permute-start = (bf16[32,264,128]{2,1,0:T(8,128)(2,1)S(1)}, bf16[32,264,128]{2,1,0:T(8,128)(2,1)S(1)}, u32[]{:S(2)}, u32[]{:S(2)}) collective-permute-start(bf16[32,264,128]{2,1,0:T(8,128)(2,1)S(1)} %all_to_all.10._.own_ref), channel_id=1, source_target_pairs={{0,4},{4,0},{1,5},{5,1},{2,6},{6,2},{3,7},{7,3},{8,12},{12,8},{9,1... | collective-permute-start | bytes 6488072 | tf_op jit(solution)/shard_map/ppermute | solution.py:266
  75.4 17.7 %collective-permute-start.2 = (bf16[1408,128]{1,0:T(8,128)(2,1)S(1)}, bf16[1408,128]{1,0:T(8,128)(2,1)S(1)}, u32[]{:S(2)}, u32[]{:S(2)}) collective-permute-start(bf16[1408,128]{1,0:T(8,128)(2,1)S(1)} %shard_map.69), channel_id=1, source_target_pairs={{0,2},{1,3},{2,0},{3,1},{4,6},{5,7},{6,4},{7,5},{8,10},{9,11},{10,... | collective-permute-start | bytes 1081352 | tf_op jit(solution)/shard_map/ppermute | solution.py:266
  76.9 16.1 %collective-permute-start.1 = (bf16[1408,128]{1,0:T(8,128)(2,1)S(1)}, bf16[1408,128]{1,0:T(8,128)(2,1)S(1)}, u32[]{:S(2)}, u32[]{:S(2)}) collective-permute-start(bf16[1408,128]{1,0:T(8,128)(2,1)S(1)} %get-tuple-element.12), channel_id=1, source_target_pairs={{0,1},{1,2},{2,3},{3,0},{4,5},{5,6},{6,7},{7,4},{8,9},{9,10},{10,1... | collective-permute-start | bytes 1081352 | tf_op jit(solution)/shard_map/ppermute | solution.py:266
  80.5 14.7 %collective-permute-start.3 = (bf16[1408,128]{1,0:T(8,128)(2,1)S(1)}, bf16[1408,128]{1,0:T(8,128)(2,1)S(1)}, u32[]{:S(2)}, u32[]{:S(2)}) collective-permute-start(bf16[1408,128]{1,0:T(8,128)(2,1)S(1)} %shard_map.71), channel_id=1, source_target_pairs={{0,3},{1,0},{2,1},{3,2},{4,7},{5,4},{6,5},{7,6},{8,11},{9,8},{10,9... | collective-permute-start | bytes 1081352 | tf_op jit(solution)/shard_map/ppermute | solution.py:266
  93.1 7.5 %copy-start.3 = (f32[900]{0:T(1024)S(1)}, f32[900]{0:T(1024)}, u32[]{:S(2)}) copy-start(f32[900]{0:T(1024)} %param.10) | copy-start | bytes 10804
  93.1 7.9 %copy-start.2 = (f32[150]{0:T(256)S(1)}, f32[150]{0:T(256)}, u32[]{:S(2)}) copy-start(f32[150]{0:T(256)} %param.9) | copy-start | bytes 1804
  93.1 22.6 %copy-start.1 = (bf16[8,22016]{1,0:T(8,128)(2,1)S(1)}, bf16[8,22016]{1,0:T(8,128)(2,1)}, u32[]{:S(2)}) copy-start(bf16[8,22016]{1,0:T(8,128)(2,1)} %rest_ref.1) | copy-start | bytes 1056772
  96.1 19.6 %all-to-all-start.1 = ((bf16[32,8,768]{2,1,0:T(8,128)(2,1)}), bf16[32,8,768]{2,1,0:T(8,128)(2,1)S(1)}, u32[]{:S(2)}, u32[]{:S(2)}) async-start(bf16[32,8,768]{2,1,0:T(8,128)(2,1)} %bitcast.7), calls=%async_computation.1 | async-start | bytes 786432 | tf_op jit(solution)/shard_map/all_to_all | solution.py:300

commit v6 on v5

--- a/solution.py
+++ b/solution.py
@@ -11,6 +11,7 @@
 CHIPS = Z * Y
 TILE, HALF = 128, 64
 WHOLE = 5
+COPIES = 4
 TILES = WHOLE + 1
 STEP = 2 * TILE
 ORDER = (1, 2, 3)
@@ -47,11 +48,22 @@
     return jnp.concatenate([block[:, HALF:], block[:, :HALF]], axis=1)
 
 
-def repack_kernel(plan, amp_ref, out_ref):
+def repack_kernel(plan, source_ref, out_ref, amp_ref, sem):
     depth = amp_ref.shape[0]
+    width = plan.tiles // COPIES
+    copies = []
+    for i in range(COPIES):
+        here = pl.ds(i * width * TILE, width * TILE)
+        copies.append(pltpu.make_async_copy(source_ref.at[:, here], amp_ref.at[:, here], sem.at[i]))
+    for copy in copies:
+        copy.start()
+    arrived = 0
     middle = depth // 2
     low = lax.broadcasted_iota(jnp.int32, (middle, TILE), 1) < HALF
     for h in range(CHIPS):
+        while arrived * width <= max(plan.first[h] + WHOLE - 1, plan.split[h]):
+            copies[arrived].wait()
+            arrived += 1
         for place in range(WHOLE):
             start = (plan.first[h] + place) * TILE
             out_ref[h, place * depth : (place + 1) * depth] = amp_ref[:, start : start + TILE]
@@ -68,10 +80,11 @@
     return pl.pallas_call(
         functools.partial(repack_kernel, plan),
         out_shape=jax.ShapeDtypeStruct((CHIPS, WHOLE * depth + depth // 2, TILE), BF16),
-        in_specs=[VMEM],
+        in_specs=[ANY],
         out_specs=VMEM,
-        compiler_params=LIMIT,
-    )(amp)
+        scratch_shapes=[pltpu.VMEM(amp.shape, BF16), pltpu.SemaphoreType.DMA((COPIES,))],
+        compiler_params=LIMIT,
+    )(pltpu.with_memory_space_constraint(amp, pltpu.HBM))
 
 
 def hold_kernel(place_ref, weight_ref, _, out_ref, sem):

time: 117 us -> 117 us (level)
  local copies, waits for them, and re-layouts: 1.96 us -> 0.36 us
  Pallas kernels: 12.3 us -> 13.6 us
    unnamed x8 -> x6, local copies, waits for them, and re-layouts: 1.61 us -> 0.02 us
    pallas_call x1, Pallas kernels: 0.39 us -> 1.75 us  [repack(): pl.pallas_call(functools.partial(repack_kernel, plan), out_shape=jax.Shap...]
where the time goes in v6:
time: 117 us; the launch traced here: 116 us
  blocking collectives  65.5 us (56%)
  waiting for transfers between devices  28.2 us (24%)
  Pallas kernels  13.6 us (12%)
  starting transfers between devices  7.56 us (6%)
    all_to_all x1, blocking collectives, on_device(): lax.all_to_all(sent, ('z', 'y'), split_axis=0, concat_axis=0, tiled=True)  65.5 us
    all_to_all x1, waiting for transfers between devices, on_device(): lax.all_to_all(total.reshape(CHIPS, share, -1), ('z', 'y'), split_axis=0,...  14.4 us
    ppermute x4, waiting for transfers between devices, shifted(): lax.ppermute(array, axis, [(i, (i + shift) % size) for i in range(size)])  13.8 us
    pallas_call x3, Pallas kernels, matmul(): pl.pallas_call(functools.partial(matmul_kernel, k), out_shape=packed(weig...  4.38 us
    all_to_all x1, starting transfers between devices, on_device(): lax.all_to_all(total.reshape(CHIPS, share, -1), ('z', 'y'), split_axis=0,...  3.88 us
    ppermute x4, starting transfers between devices, shifted(): lax.ppermute(array, axis, [(i, (i + shift) % size) for i in range(size)])  3.67 us
    pallas_call x1, Pallas kernels, hold(): pl.pallas_call(hold_kernel, out_shape=jax.ShapeDtypeStruct((REPS, chips,...  3.42 us
  transfers between devices with their start and end apart: 5, of which 4 were waited for; matrix products, arithmetic and copies ran while one was open for 1% of the time, Pallas kernels for 6%

profile of v6, /device:TPU:6, one launch (start us, length us, event | category | flops | bytes accessed | tf_op | source)
XLA Modules:
  0.0 116.4 jit_solution(7192081106344860161)
XLA Ops:
  0.0 1.8 %shard_map.64 = bf16[32,264,128]{2,1,0:T(8,128)(2,1)S(1)} custom-call(bf16[48,22016]{1,0:T(8,128)(2,1)} %bitcast.15), custom_call_target="tpu_custom_call" | custom-call | tf_op jit(solution)/shard_map/pallas_call | solution.py:80
  1.8 0.1 pad_add_fusion.place_ref
  1.8 65.5 %all_to_all.10._.own_ref = bf16[32,264,128]{2,1,0:T(8,128)(2,1)S(1)} all-to-all(bf16[32,264,128]{2,1,0:T(8,128)(2,1)S(1)} %shard_map.64), channel_id=1, replica_groups=mesh['z'=8,'y'=4,'core'=2,'rep'=4] {'z','y'}, dimensions={0} | all-to-all | bytes 4325376 | tf_op jit(solution)/shard_map/all_to_all | solution.py:309
  67.3 3.4 %shard_map.65.weight_ref = bf16[4,32,8,3072]{3,2,1,0:T(8,128)(2,1)S(1)} custom-call(s32[4]{0:T(128)S(1)} %pad_add_fusion.place_ref, bf16[32,2,4,8,3072]{4,3,2,1,0:T(8,128)(2,1)} %bitcast.14, bf16[32,264,128]{2,1,0:T(8,128)(2,1)S(1)} %all_to_all.10._.own_ref), custom_call_target="tpu_custom_call" | custom-call | tf_op jit(solution)/shard_map/pallas_call | solution.py:106
  70.7 0.8 collective-permute-done.other_ref
  71.6 2.2 %shard_map.66 = (bf16[32,2,48,768]{3,2,1,0:T(8,128)(2,1)S(1)}, bf16[1408,128]{1,0:T(8,128)(2,1)S(1)}) custom-call(s32[4]{0:T(128)S(1)} %pad_add_fusion.place_ref, bf16[32,264,128]{2,1,0:T(8,128)(2,1)S(1)} %all_to_all.10._.own_ref, bf16[32,264,128]{2,1,0:T(8,128)(2,1)S(1)} %collective-permute-done.other_ref, bf16[4,32,8,3072]{3,2,1,0:T(8,128)(2,1)S(1)} %shard_map.65.weight_ref), custom_call_target="tpu_custom_call" | custom-call | flops 1207959552 | bytes 1572864 | tf_op jit(solution)/shard_map/pallas_call | solution.py:177
  73.7 1.5 %shard_map.69 = bf16[1408,128]{1,0:T(8,128)(2,1)S(1)} custom-call(bf16[32,2,48,768]{3,2,1,0:T(8,128)(2,1)S(1)} %get-tuple-element.11.rows_ref, bf16[4,32,8,3072]{3,2,1,0:T(8,128)(2,1)S(1)} %shard_map.65.weight_ref), custom_call_target="tpu_custom_call" | custom-call | flops 1207959552 | bytes 1572864 | tf_op jit(solution)/shard_map/pallas_call | solution.py:193
  75.2 1.5 %collective-permute-start.2 = (bf16[1408,128]{1,0:T(8,128)(2,1)S(1)}, bf16[1408,128]{1,0:T(8,128)(2,1)S(1)}, u32[]{:S(2)}, u32[]{:S(2)}) collective-permute-start(bf16[1408,128]{1,0:T(8,128)(2,1)S(1)} %shard_map.69), channel_id=1, source_target_pairs={{0,2},{1,3},{2,0},{3,1},{4,6},{5,7},{6,4},{7,5},{8,10},{9,11},{10,... | collective-permute-start | bytes 1081352 | tf_op jit(solution)/shard_map/ppermute | solution.py:279
  76.7 2.1 %collective-permute-start.1 = (bf16[1408,128]{1,0:T(8,128)(2,1)S(1)}, bf16[1408,128]{1,0:T(8,128)(2,1)S(1)}, u32[]{:S(2)}, u32[]{:S(2)}) collective-permute-start(bf16[1408,128]{1,0:T(8,128)(2,1)S(1)} %get-tuple-element.12), channel_id=1, source_target_pairs={{0,1},{1,2},{2,3},{3,0},{4,5},{5,6},{6,7},{7,4},{8,9},{9,10},{10,1... | collective-permute-start | bytes 1081352 | tf_op jit(solution)/shard_map/ppermute | solution.py:279
  78.8 1.5 %shard_map.71 = bf16[1408,128]{1,0:T(8,128)(2,1)S(1)} custom-call(bf16[32,2,48,768]{3,2,1,0:T(8,128)(2,1)S(1)} %get-tuple-element.11.rows_ref, bf16[4,32,8,3072]{3,2,1,0:T(8,128)(2,1)S(1)} %shard_map.65.weight_ref), custom_call_target="tpu_custom_call" | custom-call | flops 1207959552 | bytes 1572864 | tf_op jit(solution)/shard_map/pallas_call | solution.py:193
  80.2 0.1 collective-permute-start.3
  80.3 1.5 %shard_map.67.total_ref = f32[1408,128]{1,0:T(8,128)S(1)} custom-call(bf16[32,2,48,768]{3,2,1,0:T(8,128)(2,1)S(1)} %get-tuple-element.11.rows_ref, bf16[4,32,8,3072]{3,2,1,0:T(8,128)(2,1)S(1)} %shard_map.65.weight_ref), custom_call_target="tpu_custom_call" | custom-call | flops 1207959552 | bytes 1572864 | tf_op jit(solution)/shard_map/pallas_call | solution.py:193
  81.8 11.0 %collective-permute-done.1.refs_0_ = bf16[1408,128]{1,0:T(8,128)(2,1)S(1)} collective-permute-done((bf16[1408,128]{1,0:T(8,128)(2,1)S(1)}, bf16[1408,128]{1,0:T(8,128)(2,1)S(1)}, u32[]{:S(2)}, u32[]{:S(2)}) %collective-permute-start.1) | collective-permute-done | bytes 360480 | tf_op jit(solution)/shard_map/ppermute | solution.py:279
  92.9 0.1 shard_map.70.total_ref
  93.0 2.0 %collective-permute-done.3.refs_0_ = bf16[1408,128]{1,0:T(8,128)(2,1)S(1)} collective-permute-done((bf16[1408,128]{1,0:T(8,128)(2,1)S(1)}, bf16[1408,128]{1,0:T(8,128)(2,1)S(1)}, u32[]{:S(2)}, u32[]{:S(2)}) %collective-permute-start.3) | collective-permute-done | bytes 360480 | tf_op jit(solution)/shard_map/ppermute | solution.py:279
  95.0 0.9 shard_map.72
  95.9 3.9 %all-to-all-start.1 = ((bf16[32,8,768]{2,1,0:T(8,128)(2,1)}), bf16[32,8,768]{2,1,0:T(8,128)(2,1)S(1)}, u32[]{:S(2)}, u32[]{:S(2)}) async-start(bf16[32,8,768]{2,1,0:T(8,128)(2,1)} %bitcast.7), calls=%async_computation.1 | async-start | bytes 786432 | tf_op jit(solution)/shard_map/all_to_all | solution.py:313
  100.4 0.2 select_reduce_fusion
  100.7 0.1 copy.8.virtual_ref
  100.8 0.1 broadcast_add_fusion
  100.9 0.2 add.73
  101.1 0.1 broadcast_in_dim.28.occupied_ref
  101.1 14.4 %all-to-all-done.1.ladder_ref = bf16[32,8,768]{2,1,0:T(8,128)(2,1)S(1)} async-done(((bf16[32,8,768]{2,1,0:T(8,128)(2,1)}), bf16[32,8,768]{2,1,0:T(8,128)(2,1)S(1)}, u32[]{:S(2)}, u32[]{:S(2)}) %all-to-all-start.1) | async-done | bytes 393248 | tf_op jit(solution)/shard_map/all_to_all | solution.py:313
  115.5 0.9 shard_map.73
  (11 shorter events, 0.1 us)
Async XLA Ops:
  67.3 4.3 %collective-permute-start = (bf16[32,264,128]{2,1,0:T(8,128)(2,1)S(1)}, bf16[32,264,128]{2,1,0:T(8,128)(2,1)S(1)}, u32[]{:S(2)}, u32[]{:S(2)}) collective-permute-start(bf16[32,264,128]{2,1,0:T(8,128)(2,1)S(1)} %all_to_all.10._.own_ref), channel_id=1, source_target_pairs={{0,4},{4,0},{1,5},{5,1},{2,6},{6,2},{3,7},{7,3},{8,12},{12,8},{9,1... | collective-permute-start | bytes 6488072 | tf_op jit(solution)/shard_map/ppermute | solution.py:279
  75.2 17.7 %collective-permute-start.2 = (bf16[1408,128]{1,0:T(8,128)(2,1)S(1)}, bf16[1408,128]{1,0:T(8,128)(2,1)S(1)}, u32[]{:S(2)}, u32[]{:S(2)}) collective-permute-start(bf16[1408,128]{1,0:T(8,128)(2,1)S(1)} %shard_map.69), channel_id=1, source_target_pairs={{0,2},{1,3},{2,0},{3,1},{4,6},{5,7},{6,4},{7,5},{8,10},{9,11},{10,... | collective-permute-start | bytes 1081352 | tf_op jit(solution)/shard_map/ppermute | solution.py:279
  76.7 16.1 %collective-permute-start.1 = (bf16[1408,128]{1,0:T(8,128)(2,1)S(1)}, bf16[1408,128]{1,0:T(8,128)(2,1)S(1)}, u32[]{:S(2)}, u32[]{:S(2)}) collective-permute-start(bf16[1408,128]{1,0:T(8,128)(2,1)S(1)} %get-tuple-element.12), channel_id=1, source_target_pairs={{0,1},{1,2},{2,3},{3,0},{4,5},{5,6},{6,7},{7,4},{8,9},{9,10},{10,1... | collective-permute-start | bytes 1081352 | tf_op jit(solution)/shard_map/ppermute | solution.py:279
  80.2 14.7 %collective-permute-start.3 = (bf16[1408,128]{1,0:T(8,128)(2,1)S(1)}, bf16[1408,128]{1,0:T(8,128)(2,1)S(1)}, u32[]{:S(2)}, u32[]{:S(2)}) collective-permute-start(bf16[1408,128]{1,0:T(8,128)(2,1)S(1)} %shard_map.71), channel_id=1, source_target_pairs={{0,3},{1,0},{2,1},{3,2},{4,7},{5,4},{6,5},{7,6},{8,11},{9,8},{10,9... | collective-permute-start | bytes 1081352 | tf_op jit(solution)/shard_map/ppermute | solution.py:279
  92.9 7.6 %copy-start.2 = (f32[900]{0:T(1024)S(1)}, f32[900]{0:T(1024)}, u32[]{:S(2)}) copy-start(f32[900]{0:T(1024)} %param.10) | copy-start | bytes 10804
  92.9 7.9 %copy-start.1 = (f32[150]{0:T(256)S(1)}, f32[150]{0:T(256)}, u32[]{:S(2)}) copy-start(f32[150]{0:T(256)} %param.9) | copy-start | bytes 1804
  92.9 22.6 %copy-start = (bf16[8,22016]{1,0:T(8,128)(2,1)S(1)}, bf16[8,22016]{1,0:T(8,128)(2,1)}, u32[]{:S(2)}) copy-start(bf16[8,22016]{1,0:T(8,128)(2,1)} %rest_ref.1) | copy-start | bytes 1056772
  95.9 19.6 %all-to-all-start.1 = ((bf16[32,8,768]{2,1,0:T(8,128)(2,1)}), bf16[32,8,768]{2,1,0:T(8,128)(2,1)S(1)}, u32[]{:S(2)}, u32[]{:S(2)}) async-start(bf16[32,8,768]{2,1,0:T(8,128)(2,1)} %bitcast.7), calls=%async_computation.1 | async-start | bytes 786432 | tf_op jit(solution)/shard_map/all_to_all | solution.py:313

commit v7 on v5

--- a/solution.py
+++ b/solution.py
@@ -14,7 +14,7 @@
 TILES = WHOLE + 1
 STEP = 2 * TILE
 ORDER = (1, 2, 3)
-PIECES = (1, 1, 1, 1)
+PIECES = (1, 1, 2, 1)
 BF16, F32 = jnp.bfloat16, jnp.float32
 ANY = pl.BlockSpec(memory_space=pl.ANY)
 VMEM = pl.BlockSpec(memory_space=pltpu.VMEM)

time: 117 us -> 117 us (level)
  waiting for transfers between devices: 28.2 us -> 25.3 us
  starting transfers between devices: 7.55 us -> 9.68 us
    ppermute x4 -> x5, waiting for transfers between devices: 13.8 us -> 11.7 us  [shifted(): lax.ppermute(array, axis, [(i, (i + shift) % size) for i in range(size)])]
    ppermute x4 -> x5, starting transfers between devices: 3.67 us -> 5.8 us  [shifted(): lax.ppermute(array, axis, [(i, (i + shift) % size) for i in range(size)])]
  transfers between devices with their start and end apart: 5 -> 6, of which waited for: 4 -> 6; matrix products, arithmetic and copies ran while one was open for 1% -> 1% of each run, Pallas kernels for 6% -> 7%
where the time goes in v7:
time: 117 us; the launch traced here: 116 us
  blocking collectives  65.5 us (56%)
  waiting for transfers between devices  25.3 us (22%)
  Pallas kernels  12.3 us (11%)
  starting transfers between devices  9.68 us (8%)
  local copies, waits for them, and re-layouts  1.96 us (2%)
    all_to_all x1, blocking collectives, on_device(): lax.all_to_all(sent, ('z', 'y'), split_axis=0, concat_axis=0, tiled=True)  65.5 us
    all_to_all x1, waiting for transfers between devices, on_device(): lax.all_to_all(total.reshape(CHIPS, share, -1), ('z', 'y'), split_axis=0,...  13.6 us
    ppermute x5, waiting for transfers between devices, shifted(): lax.ppermute(array, axis, [(i, (i + shift) % size) for i in range(size)])  11.7 us
    ppermute x5, starting transfers between devices, shifted(): lax.ppermute(array, axis, [(i, (i + shift) % size) for i in range(size)])  5.8 us
    pallas_call x3, Pallas kernels, matmul(): pl.pallas_call(functools.partial(matmul_kernel, k), out_shape=packed(weig...  4.38 us
    all_to_all x1, starting transfers between devices, on_device(): lax.all_to_all(total.reshape(CHIPS, share, -1), ('z', 'y'), split_axis=0,...  3.88 us
    pallas_call x1, Pallas kernels, hold(): pl.pallas_call(hold_kernel, out_shape=jax.ShapeDtypeStruct((REPS, chips,...  3.42 us
  transfers between devices with their start and end apart: 6, of which 6 were waited for; matrix products, arithmetic and copies ran while one was open for 1% of the time, Pallas kernels for 7%

profile of v7, /device:TPU:6, one launch (start us, length us, event | category | flops | bytes accessed | tf_op | source)
XLA Modules:
  0.0 115.8 jit_solution(192762629793535419)
XLA Ops:
  0.0 1.6 %copy-done = bf16[22016,1,48]{0,2,1:T(8,128)(2,1)S(1)} copy-done((bf16[22016,1,48]{0,2,1:T(8,128)(2,1)S(1)}, bf16[22016,1,48]{0,2,1:T(8,128)(2,1)}, u32[]{:S(2)}) %copy-start) | copy-done | bytes 2113560
  1.6 0.4 shard_map.64
  2.1 65.5 %all_to_all.10._.own_ref = bf16[32,264,128]{2,1,0:T(8,128)(2,1)S(1)} all-to-all(bf16[32,264,128]{2,1,0:T(8,128)(2,1)S(1)} %shard_map.64), channel_id=1, replica_groups=mesh['z'=8,'y'=4,'core'=2,'rep'=4] {'z','y'}, dimensions={0} | all-to-all | bytes 4325376 | tf_op jit(solution)/shard_map/all_to_all | solution.py:296
  67.5 3.4 %shard_map.65.weight_ref = bf16[4,32,8,3072]{3,2,1,0:T(8,128)(2,1)S(1)} custom-call(s32[4]{0:T(128)S(1)} %pad_add_fusion.place_ref, bf16[32,2,4,8,3072]{4,3,2,1,0:T(8,128)(2,1)} %bitcast.15, bf16[32,264,128]{2,1,0:T(8,128)(2,1)S(1)} %all_to_all.10._.own_ref), custom_call_target="tpu_custom_call" | custom-call | tf_op jit(solution)/shard_map/pallas_call | solution.py:93
  71.0 0.8 collective-permute-done.other_ref
  71.8 2.2 %shard_map.66 = (bf16[32,2,48,768]{3,2,1,0:T(8,128)(2,1)S(1)}, bf16[1408,128]{1,0:T(8,128)(2,1)S(1)}) custom-call(s32[4]{0:T(128)S(1)} %pad_add_fusion.place_ref, bf16[32,264,128]{2,1,0:T(8,128)(2,1)S(1)} %all_to_all.10._.own_ref, bf16[32,264,128]{2,1,0:T(8,128)(2,1)S(1)} %collective-permute-done.other_ref, bf16[4,32,8,3072]{3,2,1,0:T(8,128)(2,1)S(1)} %shard_map.65.weight_ref), custom_call_target="tpu_custom_call" | custom-call | flops 1207959552 | bytes 1572864 | tf_op jit(solution)/shard_map/pallas_call | solution.py:164
  74.0 0.6 collective-permute-start.1
  74.5 1.5 %shard_map.71 = bf16[1408,128]{1,0:T(8,128)(2,1)S(1)} custom-call(bf16[32,2,48,768]{3,2,1,0:T(8,128)(2,1)S(1)} %get-tuple-element.13.rows_ref, bf16[4,32,8,3072]{3,2,1,0:T(8,128)(2,1)S(1)} %shard_map.65.weight_ref), custom_call_target="tpu_custom_call" | custom-call | flops 1207959552 | bytes 1572864 | tf_op jit(solution)/shard_map/pallas_call | solution.py:180
  76.0 1.6 %collective-permute-start.4 = (bf16[1408,128]{1,0:T(8,128)(2,1)S(1)}, bf16[1408,128]{1,0:T(8,128)(2,1)S(1)}, u32[]{:S(2)}, u32[]{:S(2)}) collective-permute-start(bf16[1408,128]{1,0:T(8,128)(2,1)S(1)} %shard_map.71), channel_id=1, source_target_pairs={{0,3},{1,0},{2,1},{3,2},{4,7},{5,4},{6,5},{7,6},{8,11},{9,8},{10,9... | collective-permute-start | bytes 1081352 | tf_op jit(solution)/shard_map/ppermute | solution.py:266
  77.6 1.5 %shard_map.69 = (bf16[704,128]{1,0:T(8,128)(2,1)S(1)}, bf16[704,128]{1,0:T(8,128)(2,1)S(1)}) custom-call(bf16[32,2,48,768]{3,2,1,0:T(8,128)(2,1)S(1)} %get-tuple-element.13.rows_ref, bf16[4,32,8,3072]{3,2,1,0:T(8,128)(2,1)S(1)} %shard_map.65.weight_ref), custom_call_target="tpu_custom_call" | custom-call | flops 1207959552 | bytes 1572864 | tf_op jit(solution)/shard_map/pallas_call | solution.py:180
  79.1 1.5 %collective-permute-start.2 = (bf16[704,128]{1,0:T(8,128)(2,1)S(1)}, bf16[704,128]{1,0:T(8,128)(2,1)S(1)}, u32[]{:S(2)}, u32[]{:S(2)}) collective-permute-start(bf16[704,128]{1,0:T(8,128)(2,1)S(1)} %get-tuple-element.15), channel_id=1, source_target_pairs={{0,2},{1,3},{2,0},{3,1},{4,6},{5,7},{6,4},{7,5},{8,10},{9,11},{10,... | collective-permute-start | bytes 540680 | tf_op jit(solution)/shard_map/ppermute | solution.py:266
  80.6 2.1 %collective-permute-start.3 = (bf16[704,128]{1,0:T(8,128)(2,1)S(1)}, bf16[704,128]{1,0:T(8,128)(2,1)S(1)}, u32[]{:S(2)}, u32[]{:S(2)}) collective-permute-start(bf16[704,128]{1,0:T(8,128)(2,1)S(1)} %get-tuple-element.16), channel_id=1, source_target_pairs={{0,2},{1,3},{2,0},{3,1},{4,6},{5,7},{6,4},{7,5},{8,10},{9,11},{10,... | collective-permute-start | bytes 540680 | tf_op jit(solution)/shard_map/ppermute | solution.py:266
  82.7 1.5 %shard_map.67.total_ref = f32[1408,128]{1,0:T(8,128)S(1)} custom-call(bf16[32,2,48,768]{3,2,1,0:T(8,128)(2,1)S(1)} %get-tuple-element.13.rows_ref, bf16[4,32,8,3072]{3,2,1,0:T(8,128)(2,1)S(1)} %shard_map.65.weight_ref), custom_call_target="tpu_custom_call" | custom-call | flops 1207959552 | bytes 1572864 | tf_op jit(solution)/shard_map/pallas_call | solution.py:180
  84.1 1.1 collective-permute-done.1.refs_0_
  85.4 6.8 %collective-permute-done.2.refs_0_ = bf16[704,128]{1,0:T(8,128)(2,1)S(1)} collective-permute-done((bf16[704,128]{1,0:T(8,128)(2,1)S(1)}, bf16[704,128]{1,0:T(8,128)(2,1)S(1)}, u32[]{:S(2)}, u32[]{:S(2)}) %collective-permute-start.2) | collective-permute-done | bytes 180256 | tf_op jit(solution)/shard_map/ppermute | solution.py:266
  92.2 2.7 %collective-permute-done.3.refs_1_ = bf16[704,128]{1,0:T(8,128)(2,1)S(1)} collective-permute-done((bf16[704,128]{1,0:T(8,128)(2,1)S(1)}, bf16[704,128]{1,0:T(8,128)(2,1)S(1)}, u32[]{:S(2)}, u32[]{:S(2)}) %collective-permute-start.3) | collective-permute-done | bytes 180256 | tf_op jit(solution)/shard_map/ppermute | solution.py:266
  95.1 0.1 collective-permute-done.4.refs_0_
  95.2 0.9 shard_map.72
  96.0 3.9 %all-to-all-start.1 = ((bf16[32,8,768]{2,1,0:T(8,128)(2,1)}), bf16[32,8,768]{2,1,0:T(8,128)(2,1)S(1)}, u32[]{:S(2)}, u32[]{:S(2)}) async-start(bf16[32,8,768]{2,1,0:T(8,128)(2,1)} %bitcast.7), calls=%async_computation.1 | async-start | bytes 786432 | tf_op jit(solution)/shard_map/all_to_all | solution.py:300
  100.6 0.2 select_reduce_fusion
  100.9 0.1 broadcast_add_fusion
  101.0 0.2 add.73
  101.3 13.6 %all-to-all-done.1.ladder_ref = bf16[32,8,768]{2,1,0:T(8,128)(2,1)S(1)} async-done(((bf16[32,8,768]{2,1,0:T(8,128)(2,1)}), bf16[32,8,768]{2,1,0:T(8,128)(2,1)S(1)}, u32[]{:S(2)}, u32[]{:S(2)}) %all-to-all-start.1) | async-done | bytes 393248 | tf_op jit(solution)/shard_map/all_to_all | solution.py:300
  114.9 0.9 shard_map.73
  (15 shorter events, 0.4 us)
Async XLA Ops:
  0.0 1.6 %copy-start = (bf16[22016,1,48]{0,2,1:T(8,128)(2,1)S(1)}, bf16[22016,1,48]{0,2,1:T(8,128)(2,1)}, u32[]{:S(2)}) copy-start(bf16[22016,1,48]{0,2,1:T(8,128)(2,1)} %param.6) | copy-start | bytes 6340612
  67.5 4.3 %collective-permute-start = (bf16[32,264,128]{2,1,0:T(8,128)(2,1)S(1)}, bf16[32,264,128]{2,1,0:T(8,128)(2,1)S(1)}, u32[]{:S(2)}, u32[]{:S(2)}) collective-permute-start(bf16[32,264,128]{2,1,0:T(8,128)(2,1)S(1)} %all_to_all.10._.own_ref), channel_id=1, source_target_pairs={{0,4},{4,0},{1,5},{5,1},{2,6},{6,2},{3,7},{7,3},{8,12},{12,8},{9,1... | collective-permute-start | bytes 6488072 | tf_op jit(solution)/shard_map/ppermute | solution.py:266
  74.0 11.3 %collective-permute-start.1 = (bf16[1408,128]{1,0:T(8,128)(2,1)S(1)}, bf16[1408,128]{1,0:T(8,128)(2,1)S(1)}, u32[]{:S(2)}, u32[]{:S(2)}) collective-permute-start(bf16[1408,128]{1,0:T(8,128)(2,1)S(1)} %get-tuple-element.14), channel_id=1, source_target_pairs={{0,1},{1,2},{2,3},{3,0},{4,5},{5,6},{6,7},{7,4},{8,9},{9,10},{10,1... | collective-permute-start | bytes 1081352 | tf_op jit(solution)/shard_map/ppermute | solution.py:266
  76.0 19.2 %collective-permute-start.4 = (bf16[1408,128]{1,0:T(8,128)(2,1)S(1)}, bf16[1408,128]{1,0:T(8,128)(2,1)S(1)}, u32[]{:S(2)}, u32[]{:S(2)}) collective-permute-start(bf16[1408,128]{1,0:T(8,128)(2,1)S(1)} %shard_map.71), channel_id=1, source_target_pairs={{0,3},{1,0},{2,1},{3,2},{4,7},{5,4},{6,5},{7,6},{8,11},{9,8},{10,9... | collective-permute-start | bytes 1081352 | tf_op jit(solution)/shard_map/ppermute | solution.py:266
  79.1 13.2 %collective-permute-start.2 = (bf16[704,128]{1,0:T(8,128)(2,1)S(1)}, bf16[704,128]{1,0:T(8,128)(2,1)S(1)}, u32[]{:S(2)}, u32[]{:S(2)}) collective-permute-start(bf16[704,128]{1,0:T(8,128)(2,1)S(1)} %get-tuple-element.15), channel_id=1, source_target_pairs={{0,2},{1,3},{2,0},{3,1},{4,6},{5,7},{6,4},{7,5},{8,10},{9,11},{10,... | collective-permute-start | bytes 540680 | tf_op jit(solution)/shard_map/ppermute | solution.py:266
  80.6 14.4 %collective-permute-start.3 = (bf16[704,128]{1,0:T(8,128)(2,1)S(1)}, bf16[704,128]{1,0:T(8,128)(2,1)S(1)}, u32[]{:S(2)}, u32[]{:S(2)}) collective-permute-start(bf16[704,128]{1,0:T(8,128)(2,1)S(1)} %get-tuple-element.16), channel_id=1, source_target_pairs={{0,2},{1,3},{2,0},{3,1},{4,6},{5,7},{6,4},{7,5},{8,10},{9,11},{10,... | collective-permute-start | bytes 540680 | tf_op jit(solution)/shard_map/ppermute | solution.py:266
  85.4 15.3 %copy-start.3 = (f32[900]{0:T(1024)S(1)}, f32[900]{0:T(1024)}, u32[]{:S(2)}) copy-start(f32[900]{0:T(1024)} %param.10) | copy-start | bytes 10804
  85.4 15.6 %copy-start.2 = (f32[150]{0:T(256)S(1)}, f32[150]{0:T(256)}, u32[]{:S(2)}) copy-start(f32[150]{0:T(256)} %param.9) | copy-start | bytes 1804
  85.4 29.5 %copy-start.1 = (bf16[8,22016]{1,0:T(8,128)(2,1)S(1)}, bf16[8,22016]{1,0:T(8,128)(2,1)}, u32[]{:S(2)}) copy-start(bf16[8,22016]{1,0:T(8,128)(2,1)} %rest_ref.1) | copy-start | bytes 1056772
  96.0 18.9 %all-to-all-start.1 = ((bf16[32,8,768]{2,1,0:T(8,128)(2,1)}), bf16[32,8,768]{2,1,0:T(8,128)(2,1)S(1)}, u32[]{:S(2)}, u32[]{:S(2)}) async-start(bf16[32,8,768]{2,1,0:T(8,128)(2,1)} %bitcast.7), calls=%async_computation.1 | async-start | bytes 786432 | tf_op jit(solution)/shard_map/all_to_all | solution.py:300

commit v8 on v5

--- a/solution.py
+++ b/solution.py
@@ -277,7 +277,7 @@
         blocks = sent if k == ORDER[0] else matmul(k, rows, weights)
         got.append([shifted(block, "rep", REPS, k) for block in blocks])
     total = matmul(0, rows, weights)[0]
-    for blocks in got[:-1]:
+    for blocks in (got[1], got[0]):
         total = add(total, blocks)
     return add(total, got[-1], last=True)
 

time: 117 us -> 117 us (level)
  transfers between devices with their start and end apart: 5 -> 5, of which waited for: 4 -> 5; matrix products, arithmetic and copies ran while one was open for 1% -> 1% of each run, Pallas kernels for 6% -> 6%
where the time goes in v8:
time: 117 us
  blocking collectives  65.5 us (56%)
  waiting for transfers between devices  28.2 us (24%)
  Pallas kernels  12.3 us (11%)
  starting transfers between devices  7.55 us (6%)
  local copies, waits for them, and re-layouts  1.96 us (2%)
    all_to_all x1, blocking collectives, on_device(): lax.all_to_all(sent, ('z', 'y'), split_axis=0, concat_axis=0, tiled=True)  65.5 us
    all_to_all x1, waiting for transfers between devices, on_device(): lax.all_to_all(total.reshape(CHIPS, share, -1), ('z', 'y'), split_axis=0,...  14.4 us
    ppermute x4, waiting for transfers between devices, shifted(): lax.ppermute(array, axis, [(i, (i + shift) % size) for i in range(size)])  13.8 us
    pallas_call x3, Pallas kernels, matmul(): pl.pallas_call(functools.partial(matmul_kernel, k), out_shape=packed(weig...  4.38 us
    all_to_all x1, starting transfers between devices, on_device(): lax.all_to_all(total.reshape(CHIPS, share, -1), ('z', 'y'), split_axis=0,...  3.88 us
    ppermute x4, starting transfers between devices, shifted(): lax.ppermute(array, axis, [(i, (i + shift) % size) for i in range(size)])  3.67 us
    pallas_call x1, Pallas kernels, hold(): pl.pallas_call(hold_kernel, out_shape=jax.ShapeDtypeStruct((REPS, chips,...  3.42 us
  transfers between devices with their start and end apart: 5, of which 5 were waited for; matrix products, arithmetic and copies ran while one was open for 1% of the time, Pallas kernels for 6%

profile of v8, /device:TPU:6, one launch (start us, length us, event | category | flops | bytes accessed | tf_op | source)
XLA Modules:
  0.0 116.7 jit_solution(385041089531031243)
XLA Ops:
  0.0 1.6 %copy-done = bf16[22016,1,48]{0,2,1:T(8,128)(2,1)S(1)} copy-done((bf16[22016,1,48]{0,2,1:T(8,128)(2,1)S(1)}, bf16[22016,1,48]{0,2,1:T(8,128)(2,1)}, u32[]{:S(2)}) %copy-start) | copy-done | bytes 2113560
  1.6 0.4 shard_map.64
  2.0 0.1 pad_add_fusion.place_ref
  2.1 65.5 %all_to_all.10._.own_ref = bf16[32,264,128]{2,1,0:T(8,128)(2,1)S(1)} all-to-all(bf16[32,264,128]{2,1,0:T(8,128)(2,1)S(1)} %shard_map.64), channel_id=1, replica_groups=mesh['z'=8,'y'=4,'core'=2,'rep'=4] {'z','y'}, dimensions={0} | all-to-all | bytes 4325376 | tf_op jit(solution)/shard_map/all_to_all | solution.py:296
  67.5 3.4 %shard_map.65.weight_ref = bf16[4,32,8,3072]{3,2,1,0:T(8,128)(2,1)S(1)} custom-call(s32[4]{0:T(128)S(1)} %pad_add_fusion.place_ref, bf16[32,2,4,8,3072]{4,3,2,1,0:T(8,128)(2,1)} %bitcast.15, bf16[32,264,128]{2,1,0:T(8,128)(2,1)S(1)} %all_to_all.10._.own_ref), custom_call_target="tpu_custom_call" | custom-call | tf_op jit(solution)/shard_map/pallas_call | solution.py:93
  71.0 0.8 collective-permute-done.other_ref
  71.8 2.2 %shard_map.66 = (bf16[32,2,48,768]{3,2,1,0:T(8,128)(2,1)S(1)}, bf16[1408,128]{1,0:T(8,128)(2,1)S(1)}) custom-call(s32[4]{0:T(128)S(1)} %pad_add_fusion.place_ref, bf16[32,264,128]{2,1,0:T(8,128)(2,1)S(1)} %all_to_all.10._.own_ref, bf16[32,264,128]{2,1,0:T(8,128)(2,1)S(1)} %collective-permute-done.other_ref, bf16[4,32,8,3072]{3,2,1,0:T(8,128)(2,1)S(1)} %shard_map.65.weight_ref), custom_call_target="tpu_custom_call" | custom-call | flops 1207959552 | bytes 1572864 | tf_op jit(solution)/shard_map/pallas_call | solution.py:164
  74.0 1.5 %shard_map.68 = bf16[1408,128]{1,0:T(8,128)(2,1)S(1)} custom-call(bf16[32,2,48,768]{3,2,1,0:T(8,128)(2,1)S(1)} %get-tuple-element.11.rows_ref, bf16[4,32,8,3072]{3,2,1,0:T(8,128)(2,1)S(1)} %shard_map.65.weight_ref), custom_call_target="tpu_custom_call" | custom-call | flops 1207959552 | bytes 1572864 | tf_op jit(solution)/shard_map/pallas_call | solution.py:180
  75.4 1.5 %collective-permute-start.1 = (bf16[1408,128]{1,0:T(8,128)(2,1)S(1)}, bf16[1408,128]{1,0:T(8,128)(2,1)S(1)}, u32[]{:S(2)}, u32[]{:S(2)}) collective-permute-start(bf16[1408,128]{1,0:T(8,128)(2,1)S(1)} %shard_map.68), channel_id=1, source_target_pairs={{0,2},{1,3},{2,0},{3,1},{4,6},{5,7},{6,4},{7,5},{8,10},{9,11},{10,... | collective-permute-start | bytes 1081352 | tf_op jit(solution)/shard_map/ppermute | solution.py:266
  76.9 2.1 %collective-permute-start.2 = (bf16[1408,128]{1,0:T(8,128)(2,1)S(1)}, bf16[1408,128]{1,0:T(8,128)(2,1)S(1)}, u32[]{:S(2)}, u32[]{:S(2)}) collective-permute-start(bf16[1408,128]{1,0:T(8,128)(2,1)S(1)} %get-tuple-element.12), channel_id=1, source_target_pairs={{0,1},{1,2},{2,3},{3,0},{4,5},{5,6},{6,7},{7,4},{8,9},{9,10},{10,1... | collective-permute-start | bytes 1081352 | tf_op jit(solution)/shard_map/ppermute | solution.py:266
  79.0 1.5 %shard_map.71 = bf16[1408,128]{1,0:T(8,128)(2,1)S(1)} custom-call(bf16[32,2,48,768]{3,2,1,0:T(8,128)(2,1)S(1)} %get-tuple-element.11.rows_ref, bf16[4,32,8,3072]{3,2,1,0:T(8,128)(2,1)S(1)} %shard_map.65.weight_ref), custom_call_target="tpu_custom_call" | custom-call | flops 1207959552 | bytes 1572864 | tf_op jit(solution)/shard_map/pallas_call | solution.py:180
  80.5 0.1 collective-permute-start.3
  80.6 1.5 %shard_map.67.total_ref = f32[1408,128]{1,0:T(8,128)S(1)} custom-call(bf16[32,2,48,768]{3,2,1,0:T(8,128)(2,1)S(1)} %get-tuple-element.11.rows_ref, bf16[4,32,8,3072]{3,2,1,0:T(8,128)(2,1)S(1)} %shard_map.65.weight_ref), custom_call_target="tpu_custom_call" | custom-call | flops 1207959552 | bytes 1572864 | tf_op jit(solution)/shard_map/pallas_call | solution.py:180
  82.0 6.3 %collective-permute-done.1.refs_0_ = bf16[1408,128]{1,0:T(8,128)(2,1)S(1)} collective-permute-done((bf16[1408,128]{1,0:T(8,128)(2,1)S(1)}, bf16[1408,128]{1,0:T(8,128)(2,1)S(1)}, u32[]{:S(2)}, u32[]{:S(2)}) %collective-permute-start.1) | collective-permute-done | bytes 360480 | tf_op jit(solution)/shard_map/ppermute | solution.py:266
  88.4 4.6 %collective-permute-done.2.refs_0_ = bf16[1408,128]{1,0:T(8,128)(2,1)S(1)} collective-permute-done((bf16[1408,128]{1,0:T(8,128)(2,1)S(1)}, bf16[1408,128]{1,0:T(8,128)(2,1)S(1)}, u32[]{:S(2)}, u32[]{:S(2)}) %collective-permute-start.2) | collective-permute-done | bytes 360480 | tf_op jit(solution)/shard_map/ppermute | solution.py:266
  93.1 2.1 %collective-permute-done.3.refs_0_ = bf16[1408,128]{1,0:T(8,128)(2,1)S(1)} collective-permute-done((bf16[1408,128]{1,0:T(8,128)(2,1)S(1)}, bf16[1408,128]{1,0:T(8,128)(2,1)S(1)}, u32[]{:S(2)}, u32[]{:S(2)}) %collective-permute-start.3) | collective-permute-done | bytes 360480 | tf_op jit(solution)/shard_map/ppermute | solution.py:266
  95.2 0.9 shard_map.72
  96.1 3.9 %all-to-all-start.1 = ((bf16[32,8,768]{2,1,0:T(8,128)(2,1)}), bf16[32,8,768]{2,1,0:T(8,128)(2,1)S(1)}, u32[]{:S(2)}, u32[]{:S(2)}) async-start(bf16[32,8,768]{2,1,0:T(8,128)(2,1)} %bitcast.7), calls=%async_computation.1 | async-start | bytes 786432 | tf_op jit(solution)/shard_map/all_to_all | solution.py:300
  100.7 0.2 select_reduce_fusion
  100.9 0.1 copy.8.virtual_ref
  101.0 0.1 broadcast_add_fusion
  101.1 0.2 add.73
  101.3 14.4 %all-to-all-done.1.ladder_ref = bf16[32,8,768]{2,1,0:T(8,128)(2,1)S(1)} async-done(((bf16[32,8,768]{2,1,0:T(8,128)(2,1)}), bf16[32,8,768]{2,1,0:T(8,128)(2,1)S(1)}, u32[]{:S(2)}, u32[]{:S(2)}) %all-to-all-start.1) | async-done | bytes 393248 | tf_op jit(solution)/shard_map/all_to_all | solution.py:300
  115.7 0.9 shard_map.73
  (13 shorter events, 0.2 us)
Async XLA Ops:
  0.0 1.6 %copy-start = (bf16[22016,1,48]{0,2,1:T(8,128)(2,1)S(1)}, bf16[22016,1,48]{0,2,1:T(8,128)(2,1)}, u32[]{:S(2)}) copy-start(bf16[22016,1,48]{0,2,1:T(8,128)(2,1)} %param.6) | copy-start | bytes 6340612
  67.5 4.3 %collective-permute-start = (bf16[32,264,128]{2,1,0:T(8,128)(2,1)S(1)}, bf16[32,264,128]{2,1,0:T(8,128)(2,1)S(1)}, u32[]{:S(2)}, u32[]{:S(2)}) collective-permute-start(bf16[32,264,128]{2,1,0:T(8,128)(2,1)S(1)} %all_to_all.10._.own_ref), channel_id=1, source_target_pairs={{0,4},{4,0},{1,5},{5,1},{2,6},{6,2},{3,7},{7,3},{8,12},{12,8},{9,1... | collective-permute-start | bytes 6488072 | tf_op jit(solution)/shard_map/ppermute | solution.py:266
  75.4 12.9 %collective-permute-start.1 = (bf16[1408,128]{1,0:T(8,128)(2,1)S(1)}, bf16[1408,128]{1,0:T(8,128)(2,1)S(1)}, u32[]{:S(2)}, u32[]{:S(2)}) collective-permute-start(bf16[1408,128]{1,0:T(8,128)(2,1)S(1)} %shard_map.68), channel_id=1, source_target_pairs={{0,2},{1,3},{2,0},{3,1},{4,6},{5,7},{6,4},{7,5},{8,10},{9,11},{10,... | collective-permute-start | bytes 1081352 | tf_op jit(solution)/shard_map/ppermute | solution.py:266
  76.9 16.1 %collective-permute-start.2 = (bf16[1408,128]{1,0:T(8,128)(2,1)S(1)}, bf16[1408,128]{1,0:T(8,128)(2,1)S(1)}, u32[]{:S(2)}, u32[]{:S(2)}) collective-permute-start(bf16[1408,128]{1,0:T(8,128)(2,1)S(1)} %get-tuple-element.12), channel_id=1, source_target_pairs={{0,1},{1,2},{2,3},{3,0},{4,5},{5,6},{6,7},{7,4},{8,9},{9,10},{10,1... | collective-permute-start | bytes 1081352 | tf_op jit(solution)/shard_map/ppermute | solution.py:266
  80.5 14.7 %collective-permute-start.3 = (bf16[1408,128]{1,0:T(8,128)(2,1)S(1)}, bf16[1408,128]{1,0:T(8,128)(2,1)S(1)}, u32[]{:S(2)}, u32[]{:S(2)}) collective-permute-start(bf16[1408,128]{1,0:T(8,128)(2,1)S(1)} %shard_map.71), channel_id=1, source_target_pairs={{0,3},{1,0},{2,1},{3,2},{4,7},{5,4},{6,5},{7,6},{8,11},{9,8},{10,9... | collective-permute-start | bytes 1081352 | tf_op jit(solution)/shard_map/ppermute | solution.py:266
  88.4 12.3 %copy-start.3 = (f32[900]{0:T(1024)S(1)}, f32[900]{0:T(1024)}, u32[]{:S(2)}) copy-start(f32[900]{0:T(1024)} %param.10) | copy-start | bytes 10804
  88.4 12.6 %copy-start.2 = (f32[150]{0:T(256)S(1)}, f32[150]{0:T(256)}, u32[]{:S(2)}) copy-start(f32[150]{0:T(256)} %param.9) | copy-start | bytes 1804
  88.4 27.3 %copy-start.1 = (bf16[8,22016]{1,0:T(8,128)(2,1)S(1)}, bf16[8,22016]{1,0:T(8,128)(2,1)}, u32[]{:S(2)}) copy-start(bf16[8,22016]{1,0:T(8,128)(2,1)} %rest_ref.1) | copy-start | bytes 1056772
  96.1 19.6 %all-to-all-start.1 = ((bf16[32,8,768]{2,1,0:T(8,128)(2,1)}), bf16[32,8,768]{2,1,0:T(8,128)(2,1)S(1)}, u32[]{:S(2)}, u32[]{:S(2)}) async-start(bf16[32,8,768]{2,1,0:T(8,128)(2,1)} %bitcast.7), calls=%async_computation.1 | async-start | bytes 786432 | tf_op jit(solution)/shard_map/all_to_all | solution.py:300
